TPU v7x, 512 devices: a whole 4x4x16 slice. The times are simulated.
512 devices in a mesh: space: 128 (over z, x, core), level: 4 (over y).
Axes of the slice: x: 4, y: 4, z: 16, core: 2. Of those that a mesh axis runs over, the one named last changes fastest.
Arguments:
- rhs: float32 [64, 4, 65536], P(None, None, ('space', 'level')), may hold values from -6 to 6
- fine_diag: bfloat16 [64, 64, 65536], P(None, None, ('space', 'level'))
- fine_off: bfloat16 [64, 2, 64, 65536], P(None, None, None, ('space', 'level')), may hold values from -0.375 to 0.375
- fine_cols: int32 [2, 65536], P(None, ('space', 'level')), may hold values from 0 to 65535, as said below
- aggregates: int32 [65536], P(('space', 'level')), may hold values from 0 to 16383, as said below
- coarse_diag: bfloat16 [64, 64, 16384], P(None, None, 'space')
- coarse_off: bfloat16 [64, 2, 64, 16384], P('level', None, None, 'space'), may hold values from -1.5 to 1.5
- coarse_cols: int32 [2, 16384], P(None, 'space'), may hold values from 0 to 16383, as said below
Outputs:
- solution: float32 [64, 4, 65536], P(None, None, ('space', 'level'))
Inputs may be any that keep to these rules, and one draw needn't show every extreme that they name: `fine_cols`: row 0 names for each cell another cell at most 64 cells before it (after it where none lies before), row 1 one at most 64 cells after it (before it where none lies after); every device's rows reach the distance 64. `coarse_cols`: as fine_cols, over coarse blocks with the distance 64. `aggregates`: cell c belongs to a coarse block of section c // 512, that is to a block numbered from (c // 512) * 128 up; every coarse block holds exactly 4 cells.
All inputs are finite; a program needn't handle non-finite values.
Results may differ from a plain program's by a relative error of at most 0.0085.
Values may be sent and summed in bfloat16 or wider, within the bound.
A program may use at most 64 MiB of HBM per device.

v0:
```python
import jax
import jax.numpy as jnp
from jax import lax
from jax.sharding import PartitionSpec as P

CSWEEPS = 3


OMEGA = 0.7


def with_halo(cells, sides, width):
    for axis, dim in sides:
        count = lax.axis_size(axis)
        ends = count - 1
        head = lax.slice_in_dim(cells, 0, width, axis=dim)
        tail = lax.slice_in_dim(cells, cells.shape[dim] - width, cells.shape[dim], axis=dim)
        cells = jnp.concatenate(
            [
                lax.ppermute(tail, axis, [(i, (i + 1) % count) for i in range(ends)]),
                cells,
                lax.ppermute(head, axis, [((i + 1) % count, i) for i in range(ends)]),
            ],
            axis=dim,
        )
    return cells


def approx_inverse(diag_blocks):
    order_size = diag_blocks.shape[0]
    identity = jnp.eye(order_size, dtype=jnp.float32)[:, :, None]
    widened = diag_blocks.astype(jnp.float32)
    pivots = jnp.sum(widened * identity, axis=1)
    inverse = (2.0 * identity * pivots[:, None, :] - widened) / (
        pivots[:, None, :] * pivots[None, :, :]
    )
    return inverse.astype(jnp.bfloat16)


def block_product(matrices, vector):
    return jnp.einsum("ijc,jrc->irc", matrices, vector, preferred_element_type=jnp.float32)


def far_product(off_blocks, neighbours):
    return jnp.einsum("ikjc,jrkc->irc", off_blocks, neighbours, preferred_element_type=jnp.float32)


def local(rhs, fine_diag, fine_off, fine_cols, aggregates, coarse_diag, coarse_off, coarse_cols):
    cell_count = rhs.shape[2]
    rim_width = cell_count // 2
    fine_local = fine_cols - (lax.axis_index(("space", "level")) * cell_count - rim_width)
    fine_inv = approx_inverse(fine_diag)

    def fine_apply(iterate):
        rounded = iterate.astype(jnp.bfloat16)
        own_term = block_product(fine_diag, rounded)
        extended = with_halo(rounded, ((("space", "level"), 2),), rim_width)
        return own_term + far_product(fine_off, extended[:, :, fine_local])

    def fine_smooth(source):
        return OMEGA * block_product(fine_inv, source.astype(jnp.bfloat16))

    iterate = fine_smooth(rhs)
    iterate = iterate + fine_smooth(rhs - fine_apply(iterate))
    residual = rhs - fine_apply(iterate)
    section = lax.axis_index("space")
    block_count = coarse_cols.shape[1]
    coarse_rim_width = block_count // 2
    coarse_local = coarse_cols - (section * block_count - coarse_rim_width)
    labels = section * block_count + jnp.arange(block_count, dtype=jnp.int32)
    member_table = (aggregates[:, None] == labels[None, :]).astype(jnp.float32)
    partial_value = jnp.einsum(
        "src,cb->srb", residual, member_table, precision=lax.Precision.HIGHEST
    )
    coarse_rhs = lax.psum(partial_value.astype(jnp.bfloat16), "level").astype(jnp.float32)
    coarse_inv = approx_inverse(coarse_diag)
    row_count = coarse_off.shape[0]
    row_start = lax.axis_index("level") * row_count
    inv_rows = lax.dynamic_slice_in_dim(coarse_inv, row_start, row_count, 0)
    diag_rows = lax.dynamic_slice_in_dim(coarse_diag, row_start, row_count, 0)
    rhs_rows = lax.dynamic_slice_in_dim(coarse_rhs, row_start, row_count, 0)
    correction = OMEGA * block_product(inv_rows, coarse_rhs.astype(jnp.bfloat16))
    for sweep_index in range(CSWEEPS - 1):
        rounded = correction.astype(jnp.bfloat16)
        extended_rows = with_halo(rounded, (("space", 2),), coarse_rim_width)
        extended = lax.all_gather(extended_rows, "level", axis=0, tiled=True)
        own_cols = extended[:, :, coarse_rim_width : coarse_rim_width + block_count]
        applied = block_product(diag_rows, own_cols) + far_product(
            coarse_off, extended[:, :, coarse_local]
        )
        shortfall = lax.all_gather(
            (rhs_rows - applied).astype(jnp.bfloat16), "level", axis=0, tiled=True
        )
        correction = correction + OMEGA * block_product(inv_rows, shortfall)
    coarse_full = lax.all_gather(
        correction.astype(jnp.bfloat16), "level", axis=0, tiled=True
    ).astype(correction.dtype)
    iterate = iterate + jnp.einsum(
        "srb,cb->src", coarse_full, member_table, precision=lax.Precision.HIGHEST
    )
    iterate = iterate + fine_smooth(rhs - fine_apply(iterate))
    return iterate


def solution(mesh):
    placed = (
        P(None, None, ("space", "level")),
        P(None, None, ("space", "level")),
        P(None, None, None, ("space", "level")),
        P(None, ("space", "level")),
        P(("space", "level")),
        P(None, None, "space"),
        P("level", None, None, "space"),
        P(None, "space"),
    )
    return jax.shard_map(
        local,
        mesh=mesh,
        in_specs=placed,
        out_specs=P(None, None, ("space", "level")),
        check_vma=False,
    )
```

profile of v0, /device:TPU:127, one launch (start us, length us, event | category | flops | bytes accessed | tf_op | source)
XLA Modules:
  0.0 283.2 jit_solution(11534783962642055993)
XLA Ops:
  7.7 3.9 %copy.114 = bf16[64,64,128]{1,0,2:T(8,128)(2,1)S(1)} copy(bf16[64,64,128]{2,1,0:T(8,128)(2,1)} %param.9) | data formatting | bytes 2097152 | tf_op args[1]
  11.7 3.8 %copy.124 = bf16[64,64,128]{1,0,2:T(8,128)(2,1)} copy(bf16[64,64,128]{2,1,0:T(8,128)(2,1)S(1)} %copy-done.8) | data formatting | bytes 2097152 | tf_op args[5]
  15.5 3.8 %multiply_reduce_fusion = (f32[64,128]{0,1:T(8,128)S(1)}, f32[64,128]{0,1:T(8,128)S(1)}) fusion(f32[64,64]{1,0:T(8,128)S(1)} %fusion.38, bf16[64,64,128]{1,0,2:T(8,128)(2,1)} %copy.124, bf16[64,64,128]{1,0,2:T(8,128)(2,1)S(1)} %copy.114), kind=kLoop, calls=%fused_computation.10 | loop fusion | flops 3129344 | bytes 2179072 | tf_op jit(solution)/shard_map/reduce_sum | solution.py:33
  19.4 1.6 fusion.2
  21.0 1.4 copy-done
  22.4 1.2 fusion.52
  23.6 4.9 %collective-permute-start = (bf16[64,4,64]{0,1,2:T(4,128)(2,1)S(1)}, bf16[64,4,64]{0,1,2:T(4,128)(2,1)}, u32[]{:S(2)}, u32[]{:S(2)}) collective-permute-start(bf16[64,4,64]{0,1,2:T(4,128)(2,1)S(1)} %get-tuple-element.17), channel_id=1, source_target_pairs={{0,1},{1,2},{2,3},{3,4},{4,5},{5,6},{6,7},{7,8},{8,9},{9,10},{10,1... | collective-permute-start | bytes 98312 | tf_op jit(solution)/shard_map/ppermute | solution.py:20
  28.5 1.9 collective-permute-start.1
  30.5 1.9 fusion.54
  32.4 2.4 convert_element_type.82
  35.6 1.6 fusion.21
  37.5 7.6 %copy.117 = bf16[64,2,64,128]{2,0,3,1:T(8,128)(2,1)} copy(bf16[64,2,64,128]{3,2,1,0:T(8,128)(2,1)} %param.10) | data formatting | bytes 4194304 | tf_op args[2]
  45.0 1.8 pad_maximum_fusion
  46.8 2.6 gather_fusion
  49.4 6.0 %fusion.53 = (bf16[64,4,128]{0,1,2:T(4,128)(2,1)S(1)}, f32[64,4,128]{0,1,2:T(4,128)}) fusion(f32[64,4,128]{0,1,2:T(4,128)S(1)} %get-tuple-element.20, bf16[64,64,128]{1,0,2:T(8,128)(2,1)} %copy-done, f32[64,4,128]{0,1,2:T(4,128)S(1)} %copy.118, f32[128,4,64]{2,1,0:T(4,128)} %fusion.54, bf16[64,4,2,128]{0,1,3,2:T(4,128)(2,1)} %bitcast.132, ...), kind=kOutput, calls=%fused_computation.92 | convolution fusion | flops 12779520 | bytes 3866624 | tf_op jit(solution)/shard_map/ijc,jrc->irc/dot_general | solution.py:41
  55.5 9.1 %collective-permute-start.2 = (bf16[64,4,64]{0,1,2:T(4,128)(2,1)S(1)}, bf16[64,4,64]{0,1,2:T(4,128)(2,1)S(1)}, u32[]{:S(2)}, u32[]{:S(2)}) collective-permute-start(bf16[64,4,64]{0,1,2:T(4,128)(2,1)S(1)} %get-tuple-element.15), channel_id=1, source_target_pairs={{0,1},{1,2},{2,3},{3,4},{4,5},{5,6},{6,7},{7,8},{8,9},{9,10},{10,1... | collective-permute-start | bytes 98312 | tf_op jit(solution)/shard_map/ppermute | solution.py:20
  64.6 2.1 collective-permute-start.3
  68.0 7.6 %collective-permute-done.3 = bf16[64,4,64]{0,1,2:T(4,128)(2,1)S(1)} collective-permute-done((bf16[64,4,64]{0,1,2:T(4,128)(2,1)S(1)}, bf16[64,4,64]{0,1,2:T(4,128)(2,1)S(1)}, u32[]{:S(2)}, u32[]{:S(2)}) %collective-permute-start.3) | collective-permute-done | bytes 32800 | tf_op jit(solution)/shard_map/ppermute | solution.py:22
  76.8 3.4 %convolution_bitcast_fusion.1 = f32[128,4,64]{2,1,0:T(4,128)S(1)} fusion(bf16[64,4,2,128]{0,1,3,2:T(4,128)(2,1)S(1)} %bitcast.128, bf16[64,2,64,128]{2,0,3,1:T(8,128)(2,1)} %copy.117), kind=kOutput, calls=%fused_computation.21 | convolution fusion | flops 8388608 | bytes 2359296 | tf_op jit(solution)/shard_map/ikjc,jrkc->irc/dot_general | solution.py:45
  81.3 1.9 fusion.90
  83.2 51.0 %all-reduce.2.cloned.1.call-done = bf16[64,4,128]{2,0,1:T(8,128)(2,1)} async-done(((bf16[64,4,128]{2,0,1:T(8,128)(2,1)}), bf16[64,4,128]{2,0,1:T(8,128)(2,1)}) %all-reduce.2.cloned.1.call-update) | async-done | bytes 65552 | tf_op jit(solution)/shard_map/psum | solution.py:75
  136.3 6.8 %collective-permute-start.4 = (bf16[16,4,64]{0,1,2:T(4,128)(2,1)}, bf16[16,4,64]{0,1,2:T(4,128)(2,1)}, u32[]{:S(2)}, u32[]{:S(2)}) collective-permute-start(bf16[16,4,64]{0,1,2:T(4,128)(2,1)} %get-tuple-element.13), channel_id=1, source_target_pairs={{0,4},{4,8},{8,12},{12,16},{16,20},{20,24},{24,28},{28,32},{32,36}... | collective-permute-start | bytes 24584 | tf_op jit(solution)/shard_map/ppermute | solution.py:20
  143.0 1.9 collective-permute-start.5
  145.0 1.8 copy.130
  146.8 5.4 %collective-permute-done.5 = bf16[16,4,64]{0,1,2:T(4,128)(2,1)} collective-permute-done((bf16[16,4,64]{0,1,2:T(4,128)(2,1)}, bf16[16,4,64]{0,1,2:T(4,128)(2,1)}, u32[]{:S(2)}, u32[]{:S(2)}) %collective-permute-start.5) | collective-permute-done | bytes 8224 | tf_op jit(solution)/shard_map/ppermute | solution.py:22
  152.2 1.8 pad_maximum_fusion.2
  154.1 1.8 copy.126
  155.8 9.3 %all_gather.15 = bf16[64,4,256]{2,1,0:T(4,128)(2,1)S(1)} all-gather(bf16[16,4,256]{2,1,0:T(4,128)(2,1)} %copy.126), channel_id=1, replica_groups=mesh['space'=128,'level'=4] {'level'}, dimensions={0}, use_global_device_ids=true | all-gather | bytes 163840 | tf_op jit(solution)/shard_map/all_gather | solution.py:86
  166.0 2.2 fusion.24
  169.3 2.7 gather_fusion.2
  171.9 2.0 convolution_bitcast_fusion.4
  175.8 9.7 %all_gather.16 = bf16[64,4,128]{2,0,1:T(8,128)(2,1)} all-gather(bf16[16,4,128]{2,0,1:T(8,128)(2,1)S(1)} %fusion.35), channel_id=1, replica_groups=mesh['space'=128,'level'=4] {'level'}, dimensions={0}, use_global_device_ids=true | all-gather | bytes 81920 | tf_op jit(solution)/shard_map/all_gather | solution.py:91
  186.4 1.4 fusion.14
  188.7 7.6 %collective-permute-start.6 = (bf16[16,4,64]{0,1,2:T(4,128)(2,1)S(1)}, bf16[16,4,64]{0,1,2:T(4,128)(2,1)S(1)}, u32[]{:S(2)}, u32[]{:S(2)}) collective-permute-start(bf16[16,4,64]{0,1,2:T(4,128)(2,1)S(1)} %get-tuple-element.11), channel_id=1, source_target_pairs={{0,4},{4,8},{8,12},{12,16},{16,20},{20,24},{24,28},{28,32},{32,36}... | collective-permute-start | bytes 24584 | tf_op jit(solution)/shard_map/ppermute | solution.py:20
  196.4 1.9 collective-permute-start.7
  198.3 1.9 fusion.88
  200.2 5.1 %collective-permute-done.7 = bf16[16,4,64]{0,1,2:T(4,128)(2,1)S(1)} collective-permute-done((bf16[16,4,64]{0,1,2:T(4,128)(2,1)S(1)}, bf16[16,4,64]{0,1,2:T(4,128)(2,1)S(1)}, u32[]{:S(2)}, u32[]{:S(2)}) %collective-permute-start.7) | collective-permute-done | bytes 8224 | tf_op jit(solution)/shard_map/ppermute | solution.py:22
  206.3 9.3 %all_gather.17 = bf16[64,4,256]{2,1,0:T(4,128)(2,1)S(1)} all-gather(bf16[16,4,256]{2,1,0:T(4,128)(2,1)} %copy.134), channel_id=1, replica_groups=mesh['space'=128,'level'=4] {'level'}, dimensions={0}, use_global_device_ids=true | all-gather | bytes 163840 | tf_op jit(solution)/shard_map/all_gather | solution.py:86
  216.5 1.7 gather_fusion.3
  218.2 2.2 fusion.22
  221.4 2.1 convolution_bitcast_fusion.3
  225.3 9.0 %all_gather.18 = bf16[64,4,128]{2,0,1:T(8,128)(2,1)S(1)} all-gather(bf16[16,4,128]{2,0,1:T(8,128)(2,1)S(1)} %fusion.34), channel_id=1, replica_groups=mesh['space'=128,'level'=4] {'level'}, dimensions={0}, use_global_device_ids=true | all-gather | bytes 81920 | tf_op jit(solution)/shard_map/all_gather | solution.py:91
  234.4 1.4 fusion.19
  236.0 9.0 %all_gather.19 = bf16[64,4,128]{2,1,0:T(4,128)(2,1)S(1)} all-gather(bf16[16,4,128]{2,1,0:T(4,128)(2,1)S(1)} %copy.141), channel_id=1, replica_groups=mesh['space'=128,'level'=4] {'level'}, dimensions={0}, use_global_device_ids=true | all-gather | bytes 81920 | tf_op jit(solution)/shard_map/all_gather | solution.py:95
  246.5 11.7 %collective-permute-start.8 = (bf16[64,4,64]{0,1,2:T(4,128)(2,1)S(1)}, bf16[64,4,64]{0,1,2:T(4,128)(2,1)S(1)}, u32[]{:S(2)}, u32[]{:S(2)}) collective-permute-start(bf16[64,4,64]{0,1,2:T(4,128)(2,1)S(1)} %get-tuple-element.9), channel_id=1, source_target_pairs={{0,1},{1,2},{2,3},{3,4},{4,5},{5,6},{6,7},{7,8},{8,9},{9,10},{10,1... | collective-permute-start | bytes 98312 | tf_op jit(solution)/shard_map/ppermute | solution.py:20
  258.2 1.9 collective-permute-start.9
  261.3 7.9 %collective-permute-done.9 = bf16[64,4,64]{0,1,2:T(4,128)(2,1)S(1)} collective-permute-done((bf16[64,4,64]{0,1,2:T(4,128)(2,1)S(1)}, bf16[64,4,64]{0,1,2:T(4,128)(2,1)S(1)}, u32[]{:S(2)}, u32[]{:S(2)}) %collective-permute-start.9) | collective-permute-done | bytes 32800 | tf_op jit(solution)/shard_map/ppermute | solution.py:22
  270.4 5.1 %fusion.4 = f32[64,4,128]{0,1,2:T(4,128)S(1)} fusion(f32[64,4,128]{0,1,2:T(4,128)S(1)} %get-tuple-element.8, bf16[64,64,128]{1,0,2:T(8,128)(2,1)} %copy-done, f32[64,4,128]{0,1,2:T(4,128)S(1)} %copy-done.6, f32[128,4,64]{2,1,0:T(4,128)S(1)} %fusion.56, bf16[64,4,2,128]{0,1,3,2:T(4,128)(2,1)S(1)} %bitcast.131, bf16[64,2,64,128]{2,0,3,1:T(8,128)(2,1)} %copy.117), kind=kOutput, calls=%fused_computation.13 | convolution fusion | flops 12746752 | bytes 3801088 | tf_op jit(solution)/shard_map/ijc,jrc->irc/dot_general | solution.py:41
  (86 shorter events, 23.1 us)
Async XLA Ops:
  6.5 5.2 %copy-start.8 = (bf16[64,64,128]{2,1,0:T(8,128)(2,1)S(1)}, bf16[64,64,128]{2,1,0:T(8,128)(2,1)}, u32[]{:S(2)}) copy-start(bf16[64,64,128]{2,1,0:T(8,128)(2,1)} %param.13) | copy-start | bytes 3145732
  6.5 127.6 %all-reduce.2.cloned.1.call-start = ((), (), s32[]{:S(2)}) async-start(), calls=%async_computation | async-start | bytes 131072 | tf_op jit(solution)/shard_map/psum | solution.py:75
  6.5 12.8 %copy-start.10 = (f32[64,64]{1,0:T(8,128)}, f32[64,64]{1,0:T(8,128)S(1)}, u32[]{:S(2)}) copy-start(f32[64,64]{1,0:T(8,128)S(1)} %fusion.39) | copy-start | bytes 49156
  19.4 13.0 %copy-start.1 = (bf16[64,64,128]{1,0,2:T(8,128)(2,1)S(1)}, bf16[64,64,128]{1,0,2:T(8,128)(2,1)}, u32[]{:S(2)}) copy-start(bf16[64,64,128]{1,0,2:T(8,128)(2,1)} %copy.124) | copy-start | bytes 3145732
  21.0 1.4 copy-start
  23.6 21.4 %collective-permute-start = (bf16[64,4,64]{0,1,2:T(4,128)(2,1)S(1)}, bf16[64,4,64]{0,1,2:T(4,128)(2,1)}, u32[]{:S(2)}, u32[]{:S(2)}) collective-permute-start(bf16[64,4,64]{0,1,2:T(4,128)(2,1)S(1)} %get-tuple-element.17), channel_id=1, source_target_pairs={{0,1},{1,2},{2,3},{3,4},{4,5},{5,6},{6,7},{7,8},{8,9},{9,10},{10,1... | collective-permute-start | bytes 98312 | tf_op jit(solution)/shard_map/ppermute | solution.py:20
  28.5 16.5 %collective-permute-start.1 = (bf16[64,4,64]{0,1,2:T(4,128)(2,1)S(1)}, bf16[64,4,64]{0,1,2:T(4,128)(2,1)}, u32[]{:S(2)}, u32[]{:S(2)}) collective-permute-start(bf16[64,4,64]{0,1,2:T(4,128)(2,1)S(1)} %get-tuple-element.18), channel_id=1, source_target_pairs={{1,0},{2,1},{3,2},{4,3},{5,4},{6,5},{7,6},{8,7},{9,8},{10,9},{11,1... | collective-permute-start | bytes 98312 | tf_op jit(solution)/shard_map/ppermute | solution.py:22
  30.4 4.4 %copy-start.14 = (s32[2,128]{1,0:T(2,128)S(1)}, s32[2,128]{1,0:T(2,128)}, u32[]{:S(2)}) copy-start(s32[2,128]{1,0:T(2,128)} %param.11) | copy-start | bytes 3076
  30.5 5.2 %copy-start.15 = (s32[2,128]{1,0:T(2,128)S(1)}, s32[2,128]{1,0:T(2,128)}, u32[]{:S(2)}) copy-start(s32[2,128]{1,0:T(2,128)} %param.15) | copy-start | bytes 3076
  32.4 4.9 %copy-start.7 = (f32[64,4,128]{2,1,0:T(4,128)S(1)}, f32[64,4,128]{2,1,0:T(4,128)}, u32[]{:S(2)}) copy-start(f32[64,4,128]{2,1,0:T(4,128)} %param.8) | copy-start | bytes 393220
  37.2 97.9 %copy-start.2 = (bf16[16,64,128]{1,0,2:T(8,128)(2,1)}, bf16[16,64,128]{1,0,2:T(8,128)(2,1)S(1)}, u32[]{:S(2)}) copy-start(bf16[16,64,128]{1,0,2:T(8,128)(2,1)S(1)} %fusion.21) | copy-start | bytes 786436
  37.3 43.1 %copy-start.12 = (s32[128]{0:T(128)}, s32[128]{0:T(128)S(1)}, u32[]{:S(2)}) copy-start(s32[128]{0:T(128)S(1)} %iota_add_fusion) | copy-start | bytes 1540
  37.4 18.0 %copy-start.5 = (f32[64,4,128]{0,1,2:T(4,128)}, f32[64,4,128]{0,1,2:T(4,128)S(1)}, u32[]{:S(2)}) copy-start(f32[64,4,128]{0,1,2:T(4,128)S(1)} %copy.118) | copy-start | bytes 393220
  55.5 12.5 %collective-permute-start.2 = (bf16[64,4,64]{0,1,2:T(4,128)(2,1)S(1)}, bf16[64,4,64]{0,1,2:T(4,128)(2,1)S(1)}, u32[]{:S(2)}, u32[]{:S(2)}) collective-permute-start(bf16[64,4,64]{0,1,2:T(4,128)(2,1)S(1)} %get-tuple-element.15), channel_id=1, source_target_pairs={{0,1},{1,2},{2,3},{3,4},{4,5},{5,6},{6,7},{7,8},{8,9},{9,10},{10,1... | collective-permute-start | bytes 98312 | tf_op jit(solution)/shard_map/ppermute | solution.py:20
  64.6 15.7 %copy-start.11 = (s32[128]{0:T(128)S(1)}, s32[128]{0:T(128)}, u32[]{:S(2)}) copy-start(s32[128]{0:T(128)} %param.12) | copy-start | bytes 1540
  64.6 11.0 %collective-permute-start.3 = (bf16[64,4,64]{0,1,2:T(4,128)(2,1)S(1)}, bf16[64,4,64]{0,1,2:T(4,128)(2,1)S(1)}, u32[]{:S(2)}, u32[]{:S(2)}) collective-permute-start(bf16[64,4,64]{0,1,2:T(4,128)(2,1)S(1)} %get-tuple-element.16), channel_id=1, source_target_pairs={{1,0},{2,1},{3,2},{4,3},{5,4},{6,5},{7,6},{8,7},{9,8},{10,9},{11,1... | collective-permute-start | bytes 98312 | tf_op jit(solution)/shard_map/ppermute | solution.py:22
  136.3 10.5 %collective-permute-start.4 = (bf16[16,4,64]{0,1,2:T(4,128)(2,1)}, bf16[16,4,64]{0,1,2:T(4,128)(2,1)}, u32[]{:S(2)}, u32[]{:S(2)}) collective-permute-start(bf16[16,4,64]{0,1,2:T(4,128)(2,1)} %get-tuple-element.13), channel_id=1, source_target_pairs={{0,4},{4,8},{8,12},{12,16},{16,20},{20,24},{24,28},{28,32},{32,36}... | collective-permute-start | bytes 24584 | tf_op jit(solution)/shard_map/ppermute | solution.py:20
  143.0 9.2 %collective-permute-start.5 = (bf16[16,4,64]{0,1,2:T(4,128)(2,1)}, bf16[16,4,64]{0,1,2:T(4,128)(2,1)}, u32[]{:S(2)}, u32[]{:S(2)}) collective-permute-start(bf16[16,4,64]{0,1,2:T(4,128)(2,1)} %get-tuple-element.14), channel_id=1, source_target_pairs={{4,0},{8,4},{12,8},{16,12},{20,16},{24,20},{28,24},{32,28},{36,32}... | collective-permute-start | bytes 24584 | tf_op jit(solution)/shard_map/ppermute | solution.py:22
  187.9 0.7 copy-start.3
  188.7 11.5 %collective-permute-start.6 = (bf16[16,4,64]{0,1,2:T(4,128)(2,1)S(1)}, bf16[16,4,64]{0,1,2:T(4,128)(2,1)S(1)}, u32[]{:S(2)}, u32[]{:S(2)}) collective-permute-start(bf16[16,4,64]{0,1,2:T(4,128)(2,1)S(1)} %get-tuple-element.11), channel_id=1, source_target_pairs={{0,4},{4,8},{8,12},{12,16},{16,20},{20,24},{24,28},{28,32},{32,36}... | collective-permute-start | bytes 24584 | tf_op jit(solution)/shard_map/ppermute | solution.py:20
  196.4 8.9 %collective-permute-start.7 = (bf16[16,4,64]{0,1,2:T(4,128)(2,1)S(1)}, bf16[16,4,64]{0,1,2:T(4,128)(2,1)S(1)}, u32[]{:S(2)}, u32[]{:S(2)}) collective-permute-start(bf16[16,4,64]{0,1,2:T(4,128)(2,1)S(1)} %get-tuple-element.12), channel_id=1, source_target_pairs={{4,0},{8,4},{12,8},{16,12},{20,16},{24,20},{28,24},{32,28},{36,32}... | collective-permute-start | bytes 24584 | tf_op jit(solution)/shard_map/ppermute | solution.py:22
  215.8 0.7 copy-start.9
  218.2 16.3 %copy-start.4 = (f32[128,4,16]{2,1,0:T(4,128)S(1)}, f32[128,4,16]{2,1,0:T(4,128)}, u32[]{:S(2)}) copy-start(f32[128,4,16]{2,1,0:T(4,128)} %copy-done.3) | copy-start | bytes 98308
  218.2 26.8 %copy-start.13 = (s32[128]{0:T(128)S(1)}, s32[128]{0:T(128)}, u32[]{:S(2)}) copy-start(s32[128]{0:T(128)} %copy-done.12) | copy-start | bytes 1540
  223.5 46.9 %copy-start.6 = (f32[64,4,128]{0,1,2:T(4,128)S(1)}, f32[64,4,128]{0,1,2:T(4,128)}, u32[]{:S(2)}) copy-start(f32[64,4,128]{0,1,2:T(4,128)} %copy-done.5) | copy-start | bytes 393220
  246.5 14.8 %collective-permute-start.8 = (bf16[64,4,64]{0,1,2:T(4,128)(2,1)S(1)}, bf16[64,4,64]{0,1,2:T(4,128)(2,1)S(1)}, u32[]{:S(2)}, u32[]{:S(2)}) collective-permute-start(bf16[64,4,64]{0,1,2:T(4,128)(2,1)S(1)} %get-tuple-element.9), channel_id=1, source_target_pairs={{0,1},{1,2},{2,3},{3,4},{4,5},{5,6},{6,7},{7,8},{8,9},{9,10},{10,1... | collective-permute-start | bytes 98312 | tf_op jit(solution)/shard_map/ppermute | solution.py:20
  258.2 11.0 %collective-permute-start.9 = (bf16[64,4,64]{0,1,2:T(4,128)(2,1)S(1)}, bf16[64,4,64]{0,1,2:T(4,128)(2,1)S(1)}, u32[]{:S(2)}, u32[]{:S(2)}) collective-permute-start(bf16[64,4,64]{0,1,2:T(4,128)(2,1)S(1)} %get-tuple-element.10), channel_id=1, source_target_pairs={{1,0},{2,1},{3,2},{4,3},{5,4},{6,5},{7,6},{8,7},{9,8},{10,9},{11,1... | collective-permute-start | bytes 98312 | tf_op jit(solution)/shard_map/ppermute | solution.py:22
Sparse Core Ops, SparseCore 0:
  81.4 52.6 all-reduce.1
where the time goes:
time: 285 us; the launch traced here: 283 us
  waiting for transfers between devices  77 us (27%)
  starting transfers between devices  49.9 us (18%)
  blocking collectives  46.2 us (16%)
  local copies, waits for them, and re-layouts  45.9 us (16%)
  matrix products  32.9 us (12%)
  other arithmetic  17.4 us (6%)
  between operations  13.9 us (5%)
    psum x1, waiting for transfers between devices, local(): lax.psum(partial_value.astype(jnp.bfloat16), 'level').astype(jnp.float32)  51 us
    ppermute x5, starting transfers between devices, with_halo(): lax.ppermute(tail, axis, [(i, (i + 1) % count) for i in range(ends)])  40.1 us
    ppermute x5, waiting for transfers between devices, with_halo(): lax.ppermute(head, axis, [((i + 1) % count, i) for i in range(ends)])  26 us
    dot_general x11, matrix products, block_product(): jnp.einsum('ijc,jrc->irc', matrices, vector, preferred_element_type=jnp.f...  24.3 us
    unnamed x37, local copies, waits for them, and re-layouts  20.1 us
    all_gather x2, blocking collectives, local(): lax.all_gather((rhs_rows - applied).astype(jnp.bfloat16), 'level', axis=0...  18.7 us
    all_gather x2, blocking collectives, local(): extended = lax.all_gather(extended_rows, 'level', axis=0, tiled=True)  18.6 us
    ppermute x5, starting transfers between devices, with_halo(): lax.ppermute(head, axis, [((i + 1) % count, i) for i in range(ends)])  9.79 us
  transfers between devices with their start and end apart: 11, of which 5 were waited for; matrix products, arithmetic and copies ran while one was open for 8% of the time, Pallas kernels for 0%

commit v1 on v0

v1 whole, which is shorter than its diff:
```python
import functools

import jax
import jax.numpy as jnp
from jax import lax
from jax.experimental import pallas as pl
from jax.experimental.pallas import tpu as pltpu
from jax.sharding import PartitionSpec as P

CSWEEPS = 3
OMEGA = 0.7
S = 64
R = 4
C = 128
HALF = 64
ROWS = 16
MESH = pl.DeviceIdType.MESH
F32 = jnp.float32
BF16 = jnp.bfloat16


def lane_low(rows):
    return lax.broadcasted_iota(jnp.int32, (rows, C), 1) < HALF


def fold_rows(parts):
    sub = lax.broadcasted_iota(jnp.int32, (8, C), 0)
    four = sub < 4
    two = lax.rem(sub, 4) < 2
    one = lax.rem(sub, 2) < 1
    level = [
        jnp.where(four, parts[i], parts[i + 4])
        + pltpu.roll(jnp.where(four, parts[i + 4], parts[i]), 4, 0)
        for i in range(4)
    ]
    level = [
        jnp.where(
            two,
            level[i] + pltpu.roll(level[i], 6, 0),
            level[i + 2] + pltpu.roll(level[i + 2], 2, 0),
        )
        for i in range(2)
    ]
    return jnp.where(
        one,
        level[0] + pltpu.roll(level[0], 7, 0),
        level[1] + pltpu.roll(level[1], 1, 0),
    )


def products(base, terms, start=None):
    sums = [[None] * R for _ in range(8)] if start is None else start
    for load, vector in terms:
        for block in range(S // 16):
            low = block * 16
            pieces = [vector[r, low : low + 16, :] for r in range(R)]
            for i in range(8):
                matrix = load(base + i, low).astype(F32)
                for r in range(R):
                    product = matrix * pieces[r]
                    piece = product[:8] + product[8:]
                    sums[i][r] = piece if sums[i][r] is None else sums[i][r] + piece
    return sums


def diag_load(ref, offset=0):
    return lambda row, low: ref[row + offset, low : low + 16, :]


def off_load(ref, first):
    def load(row, low):
        return jnp.where(
            lane_low(16),
            ref[row, first, low : low + 16, :],
            ref[row, 1 - first, low : low + 16, :],
        )

    return load


def apply_first(count, diag_ref, row_start, off_ref, vector, near, acc):
    def step(block, carry):
        base = block * 8
        sums = products(
            base,
            [(diag_load(diag_ref, row_start), vector), (off_load(off_ref, 1), near)],
        )
        for i in range(8):
            for r in range(R):
                acc[block, i * R + r] = sums[i][r]
        return carry

    lax.fori_loop(0, count // 8, step, 0)


def apply_last(count, off_ref, far, acc, out):
    def step(block, carry):
        start = [[acc[block, i * R + r] for r in range(R)] for i in range(8)]
        sums = products(block * 8, [(off_load(off_ref, 0), far)], start)
        low = pl.multiple_of(block * 8, 8)
        for r in range(R):
            out[r, pl.ds(low, 8), :] = fold_rows([sums[i][r] for i in range(8)])
        return carry

    lax.fori_loop(0, count // 8, step, 0)


def smooth(diag_ref, scale, field, scaled, out):
    for r in range(R):
        scaled[r] = field[r] * scale[...]

    def step(block, carry):
        base = block * 8
        sums = products(base, [(diag_load(diag_ref), scaled)])
        low = pl.multiple_of(base, 8)
        rows = pl.ds(low, 8)
        for r in range(R):
            total = fold_rows([sums[i][r] for i in range(8)])
            out[r, rows, :] = (OMEGA * scale[rows, :]) * (2.0 * field[r, rows, :] - total)
        return carry

    lax.fori_loop(0, S // 8, step, 0)


def pivot_scale(diag_ref, scale):
    sub = lax.broadcasted_iota(jnp.int32, (16, C), 0)

    def step(block, carry):
        low = pl.multiple_of(block * 16, 16)
        total = jnp.zeros((16, C), F32)
        for i in range(16):
            row = diag_ref[low + i, pl.ds(low, 16), :].astype(F32)
            total = jnp.where(sub == i, row, total)
        scale[pl.ds(low, 16), :] = 1.0 / total
        return carry

    lax.fori_loop(0, S // 16, step, 0)


def one_hot(cells, width):
    return (lax.broadcasted_iota(jnp.int32, (width, C), 0) == cells).astype(F32).astype(BF16)


def flat(field):
    return field.reshape(R * S, C)


def split_dot(field, matrix, dims):
    high = field.astype(BF16)
    low = (field - high.astype(F32)).astype(BF16)
    dot = lambda part: lax.dot_general(part, matrix, (dims, ((), ())), preferred_element_type=F32)
    return dot(high) + dot(low)


def kernel(
    sizes,
    rhs_hbm, diag_hbm, off_hbm, cols_ref, agg_ref, cdiag_hbm, coff_hbm, ccols_ref,
    out_ref,
    rhs_in, diag, off, cdiag, coff,
    b, x, q, u, d, xb, near, far, acc, scale, cscale, cb, e,
    hot_near, hot_far, chot_near, chot_far, member,
    send_fine, get_fine, send_coarse, get_coarse,
    send_part, get_part, send_short, get_short,
    load_sem, fine_send, fine_get, coarse_send, coarse_get,
    part_send, part_get, short_send, short_get,
):
    spaces, levels = sizes
    space = lax.axis_index("space")
    level = lax.axis_index("level")
    index = space * levels + level
    count = spaces * levels
    after = lax.rem(index + 1, count)
    before = lax.rem(index + count - 1, count)
    fine_next = (lax.div(after, levels), lax.rem(after, levels))
    fine_last = (lax.div(before, levels), lax.rem(before, levels))
    space_next = (lax.rem(space + 1, spaces), level)
    space_last = (lax.rem(space + spaces - 1, spaces), level)
    peers = [(space, lax.rem(level + k, levels)) for k in range(1, levels)]

    barrier = pltpu.get_barrier_semaphore()
    partners = [fine_next, fine_last, space_next, space_last] + peers
    for partner in partners:
        pl.semaphore_signal(barrier, inc=1, device_id=partner, device_id_type=MESH)

    loads = [
        pltpu.make_async_copy(source, target, load_sem.at[k])
        for k, (source, target) in enumerate(
            [(rhs_hbm, rhs_in), (diag_hbm, diag), (off_hbm, off), (cdiag_hbm, cdiag), (coff_hbm, coff)]
        )
    ]
    for load in loads:
        load.start()

    def remote(source, target, sent, got, device):
        return pltpu.make_async_remote_copy(
            src_ref=source, dst_ref=target, send_sem=sent, recv_sem=got,
            device_id=device, device_id_type=MESH,
        )

    low_lane = lax.broadcasted_iota(jnp.int32, (1, C), 1) < HALF

    def tables(cols, first, near_table, far_table):
        place = cols - first
        own = jnp.where(low_lane, place[1:2], place[0:1])
        reach = jnp.where(low_lane, place[0:1], place[1:2])
        near_table[...] = one_hot(own, C)
        left = jnp.where(reach < 0, reach + HALF, -1)
        right = jnp.where(reach >= C, reach - HALF, -1)
        rim = jnp.maximum(left, right)
        swapped = jnp.where(rim < 0, rim, lax.rem(rim + HALF, C))
        far_table[0, 0:C] = one_hot(rim, C)
        far_table[1, 0:C] = one_hot(swapped, C)
        inner = one_hot(reach, C)
        far_table[0, C:] = inner
        far_table[1, C:] = inner

    tables(cols_ref[...], index * C, hot_near, hot_far)
    tables(ccols_ref[...], space * C, chot_near, chot_far)
    member[...] = one_hot(agg_ref[...] - space * C, C)

    def start_rims(field, sends, gets, send_sems, get_sems, devices):
        rounded = flat(field[...]).astype(BF16)
        xb[...] = rounded
        wide = rounded.astype(F32)
        for r in range(R):
            d[r] = wide[r * S : (r + 1) * S]
        lower, upper = wide[: R * S // 2], wide[R * S // 2 :]
        turned = pltpu.roll(lower, HALF, 1)
        mask = lane_low(R * S // 2)
        sends[0] = jnp.where(mask, turned, upper).astype(BF16)
        sends[1] = jnp.where(mask, upper, turned).astype(BF16)
        copies = [
            remote(sends.at[k], gets.at[k], send_sems.at[k], get_sems.at[k], devices[k])
            for k in range(2)
        ]
        for copy in copies:
            copy.start()
        return copies

    def gather_near(table):
        near[...] = jnp.dot(xb[...], table[...], preferred_element_type=F32).reshape(R, S, C)

    def gather_far(gets, table):
        mask = lane_low(R * S // 2)
        from_left, from_right = gets[0].astype(F32), gets[1].astype(F32)
        half = R * S // 2
        for k in range(2):
            rim = jnp.where(mask, from_left, from_right) if k == 0 else jnp.where(mask, from_right, from_left)
            own = xb[k * half : (k + 1) * half]
            value = jnp.dot(rim.astype(BF16), table[k, 0:C], preferred_element_type=F32) + jnp.dot(
                own, table[k, C:], preferred_element_type=F32
            )
            far[k * R // 2 : (k + 1) * R // 2] = value.reshape(R // 2, S, C)

    waiting = []

    def fine_residual(phase):
        copies = start_rims(
            x, send_fine.at[phase], get_fine.at[phase],
            fine_send.at[phase], fine_get.at[phase], (fine_next, fine_last),
        )
        waiting.extend(copies)
        gather_near(hot_near)
        if phase == 0:
            loads[2].wait()
        apply_first(S, diag, 0, off, d, near, acc)
        for copy in copies:
            copy.wait_recv()
        gather_far(get_fine.at[phase], hot_far)
        apply_last(S, off, far, acc, q)
        q[...] = b[...] - q[...]

    loads[0].wait()
    for r in range(R):
        b[r] = rhs_in[:, r, :]
    loads[1].wait()
    pivot_scale(diag, scale)
    smooth(diag, scale, b, u, x)
    pl.semaphore_wait(barrier, len(partners))

    fine_residual(0)
    smooth(diag, scale, q, u, d)
    x[...] = x[...] + d[...]
    fine_residual(1)

    send_part[...] = split_dot(flat(q[...]), member[...], ((1,), (1,))).astype(BF16)
    parts = [
        remote(send_part, get_part.at[k], part_send.at[k], part_get.at[k], peer)
        for k, peer in enumerate(peers)
    ]
    for copy in parts:
        copy.start()
    waiting.extend(parts)
    loads[3].wait()
    loads[4].wait()
    pivot_scale(cdiag, cscale)
    for copy in parts:
        copy.wait_recv()
    total = send_part[...].astype(F32)
    for k in range(levels - 1):
        total = total + get_part[k].astype(F32)
    cb[...] = total.reshape(R, S, C)

    smooth(cdiag, cscale, cb, u, e)
    row_start = pl.multiple_of(level * ROWS, ROWS)
    for sweep in range(CSWEEPS - 1):
        copies = start_rims(
            e, send_coarse.at[sweep], get_coarse.at[sweep],
            coarse_send.at[sweep], coarse_get.at[sweep], (space_next, space_last),
        )
        waiting.extend(copies)
        gather_near(chot_near)
        apply_first(ROWS, cdiag, row_start, coff, d, near, acc)
        for copy in copies:
            copy.wait_recv()
        gather_far(get_coarse.at[sweep], chot_far)
        apply_last(ROWS, coff, far, acc, q)
        for r in range(R):
            send_short[sweep, r] = (cb[r, pl.ds(row_start, ROWS), :] - q[r, 0:ROWS, :]).astype(BF16)
        copies = [
            remote(
                send_short.at[sweep], get_short.at[sweep, k],
                short_send.at[sweep, k], short_get.at[sweep, k], peer,
            )
            for k, peer in enumerate(peers)
        ]
        for copy in copies:
            copy.start()
        waiting.extend(copies)
        for r in range(R):
            q[r, pl.ds(row_start, ROWS), :] = send_short[sweep, r].astype(F32)
        for k, copy in enumerate(copies):
            copy.wait_recv()
            source = lax.rem(level + levels - (k + 1), levels)
            rows = pl.ds(pl.multiple_of(source * ROWS, ROWS), ROWS)
            for r in range(R):
                q[r, rows, :] = get_short[sweep, k, r].astype(F32)
        smooth(cdiag, cscale, q, u, d)
        e[...] = e[...] + d[...]

    x[...] = x[...] + split_dot(flat(e[...]), member[...], ((1,), (0,))).reshape(R, S, C)
    fine_residual(2)
    smooth(diag, scale, q, u, d)
    out_ref[...] = x[...] + d[...]
    for copy in waiting:
        copy.wait_send()


def local(sizes, rhs, fine_diag, fine_off, fine_cols, aggregates, coarse_diag, coarse_off, coarse_cols):
    levels = sizes[1]
    vmem = pl.BlockSpec(memory_space=pltpu.VMEM)
    hbm = pl.BlockSpec(memory_space=pl.ANY)
    field = pltpu.VMEM((R, S, C), F32)
    dma = pltpu.SemaphoreType.DMA
    half = R * S // 2
    sweeps = CSWEEPS - 1
    result = pl.pallas_call(
        functools.partial(kernel, sizes),
        out_shape=jax.ShapeDtypeStruct((R, S, C), F32),
        in_specs=[hbm, hbm, hbm, vmem, vmem, hbm, hbm, vmem],
        out_specs=vmem,
        scratch_shapes=[
            pltpu.VMEM((S, R, C), F32),
            pltpu.VMEM((S, S, C), BF16),
            pltpu.VMEM((S, 2, S, C), BF16),
            pltpu.VMEM((S, S, C), BF16),
            pltpu.VMEM((ROWS, 2, S, C), BF16),
            field, field, field, field, field,
            pltpu.VMEM((R * S, C), BF16),
            field, field,
            pltpu.VMEM((S // 8, 8 * R, 8, C), F32),
            pltpu.VMEM((S, C), F32),
            pltpu.VMEM((S, C), F32),
            field, field,
            pltpu.VMEM((C, C), BF16),
            pltpu.VMEM((2, 2 * C, C), BF16),
            pltpu.VMEM((C, C), BF16),
            pltpu.VMEM((2, 2 * C, C), BF16),
            pltpu.VMEM((C, C), BF16),
            pltpu.VMEM((3, 2, half, C), BF16),
            pltpu.VMEM((3, 2, half, C), BF16),
            pltpu.VMEM((sweeps, 2, half, C), BF16),
            pltpu.VMEM((sweeps, 2, half, C), BF16),
            pltpu.VMEM((R * S, C), BF16),
            pltpu.VMEM((levels - 1, R * S, C), BF16),
            pltpu.VMEM((sweeps, R, ROWS, C), BF16),
            pltpu.VMEM((sweeps, levels - 1, R, ROWS, C), BF16),
            dma((5,)),
            dma((3, 2)),
            dma((3, 2)),
            dma((sweeps, 2)),
            dma((sweeps, 2)),
            dma((levels - 1,)),
            dma((levels - 1,)),
            dma((sweeps, levels - 1)),
            dma((sweeps, levels - 1)),
        ],
        compiler_params=pltpu.CompilerParams(
            collective_id=0, has_side_effects=True, vmem_limit_bytes=48 * 1024 * 1024
        ),
        name="vcycle",
    )(
        rhs, fine_diag, fine_off, fine_cols, aggregates.reshape(1, C),
        coarse_diag, coarse_off, coarse_cols,
    )
    return result.transpose(1, 0, 2)


def solution(mesh):
    placed = (
        P(None, None, ("space", "level")),
        P(None, None, ("space", "level")),
        P(None, None, None, ("space", "level")),
        P(None, ("space", "level")),
        P(("space", "level")),
        P(None, None, "space"),
        P("level", None, None, "space"),
        P(None, "space"),
    )
    sizes = (mesh.shape["space"], mesh.shape["level"])
    return jax.shard_map(
        functools.partial(local, sizes),
        mesh=mesh,
        in_specs=placed,
        out_specs=P(None, None, ("space", "level")),
        check_vma=False,
    )
```

time: 285 us -> 66.7 us (0.23)
  the two profiles are of different devices: /device:TPU:127 before, /device:TPU:1 now
where the time goes in v1:
time: 66.7 us; the launch traced here: 66.4 us
  Pallas kernels  57.6 us (86%)
  local copies, waits for them, and re-layouts  8.74 us (13%)
    pallas_call x1, Pallas kernels, local(): pl.pallas_call(functools.partial(kernel, sizes), out_shape=jax.ShapeDtype...  57.6 us
    unnamed x16, local copies, waits for them, and re-layouts  8 us

profile of v1, /device:TPU:1, one launch (start us, length us, event | category | flops | bytes accessed | tf_op | source)
XLA Modules:
  0.0 66.4 jit_solution(1255512254107662585)
XLA Ops:
  0.0 0.0 copy-start
  0.0 1.6 %copy-done = bf16[64,2,64,128]{3,2,1,0:T(8,128)(2,1)S(1)} copy-done((bf16[64,2,64,128]{3,2,1,0:T(8,128)(2,1)S(1)}, bf16[64,2,64,128]{3,2,1,0:T(8,128)(2,1)}, u32[]{:S(2)}) %copy-start) | copy-done | bytes 2097176
  1.6 0.0 copy-start.1
  1.6 1.2 %copy-done.1 = bf16[64,64,128]{2,1,0:T(8,128)(2,1)S(1)} copy-done((bf16[64,64,128]{2,1,0:T(8,128)(2,1)S(1)}, bf16[64,64,128]{2,1,0:T(8,128)(2,1)}, u32[]{:S(2)}) %copy-start.1) | copy-done | bytes 1048600
  2.8 0.0 copy-start.2
  2.8 1.2 %copy-done.2 = bf16[64,64,128]{2,1,0:T(8,128)(2,1)S(1)} copy-done((bf16[64,64,128]{2,1,0:T(8,128)(2,1)S(1)}, bf16[64,64,128]{2,1,0:T(8,128)(2,1)}, u32[]{:S(2)}) %copy-start.2) | copy-done | bytes 1048600
  4.0 0.0 copy-start.3
  4.0 1.0 %copy-done.3 = bf16[16,2,64,128]{3,2,1,0:T(8,128)(2,1)S(1)} copy-done((bf16[16,2,64,128]{3,2,1,0:T(8,128)(2,1)S(1)}, bf16[16,2,64,128]{3,2,1,0:T(8,128)(2,1)}, u32[]{:S(2)}) %copy-start.3) | copy-done | bytes 524312
  5.1 0.0 copy-start.4
  5.1 0.9 %copy-done.4 = f32[64,4,128]{2,1,0:T(4,128)S(1)} copy-done((f32[64,4,128]{2,1,0:T(4,128)S(1)}, f32[64,4,128]{2,1,0:T(4,128)}, u32[]{:S(2)}) %copy-start.4) | copy-done | bytes 131096
  6.0 0.0 copy-start.5
  6.0 0.7 %copy-done.5 = s32[2,128]{1,0:T(2,128)S(1)} copy-done((s32[2,128]{1,0:T(2,128)S(1)}, s32[2,128]{1,0:T(2,128)}, u32[]{:S(2)}) %copy-start.5) | copy-done | bytes 1048
  6.7 0.0 copy-start.6
  6.7 0.7 %copy-done.6 = s32[2,128]{1,0:T(2,128)S(1)} copy-done((s32[2,128]{1,0:T(2,128)S(1)}, s32[2,128]{1,0:T(2,128)}, u32[]{:S(2)}) %copy-start.6) | copy-done | bytes 1048
  7.3 0.0 copy-start.7
  7.4 0.7 copy-done.7
  8.0 57.6 %vcycle.1 = f32[4,64,128]{2,1,0:T(8,128)S(1)} custom-call(f32[64,4,128]{2,1,0:T(4,128)S(1)} %copy-done.4, bf16[64,64,128]{2,1,0:T(8,128)(2,1)S(1)} %copy-done.1, bf16[64,2,64,128]{3,2,1,0:T(8,128)(2,1)S(1)} %copy-done, s32[2,128]{1,0:T(2,128)S(1)} %copy-done.5, s32[1,128]{1,0:T(1,128)S(1)} %bitcast.3, bf16[64,64,128]{2,1,0:T(8,128)(2,1)S(1)} %copy-done.2, ...), custom_call_target="tpu_custom_call" | custom-call | tf_op jit(solution)/shard_map/vcycle/pallas_call | solution.py:357
  65.6 0.7 %copy.9 = f32[64,4,128]{2,1,0:T(4,128)} copy(f32[64,4,128]{2,0,1:T(8,128)S(1)} %bitcast.2) | data formatting | bytes 262144 | tf_op jit(solution)/shard_map/transpose | solution.py:406
Async XLA Ops:
  0.0 1.6 %copy-start = (bf16[64,2,64,128]{3,2,1,0:T(8,128)(2,1)S(1)}, bf16[64,2,64,128]{3,2,1,0:T(8,128)(2,1)}, u32[]{:S(2)}) copy-start(bf16[64,2,64,128]{3,2,1,0:T(8,128)(2,1)} %off_hbm.1) | copy-start | bytes 6291460
  1.6 1.2 %copy-start.1 = (bf16[64,64,128]{2,1,0:T(8,128)(2,1)S(1)}, bf16[64,64,128]{2,1,0:T(8,128)(2,1)}, u32[]{:S(2)}) copy-start(bf16[64,64,128]{2,1,0:T(8,128)(2,1)} %diag_hbm.1) | copy-start | bytes 3145732
  2.8 1.2 %copy-start.2 = (bf16[64,64,128]{2,1,0:T(8,128)(2,1)S(1)}, bf16[64,64,128]{2,1,0:T(8,128)(2,1)}, u32[]{:S(2)}) copy-start(bf16[64,64,128]{2,1,0:T(8,128)(2,1)} %cdiag_hbm.1) | copy-start | bytes 3145732
  4.0 1.0 %copy-start.3 = (bf16[16,2,64,128]{3,2,1,0:T(8,128)(2,1)S(1)}, bf16[16,2,64,128]{3,2,1,0:T(8,128)(2,1)}, u32[]{:S(2)}) copy-start(bf16[16,2,64,128]{3,2,1,0:T(8,128)(2,1)} %coff_hbm.1) | copy-start | bytes 1572868
  5.1 0.9 %copy-start.4 = (f32[64,4,128]{2,1,0:T(4,128)S(1)}, f32[64,4,128]{2,1,0:T(4,128)}, u32[]{:S(2)}) copy-start(f32[64,4,128]{2,1,0:T(4,128)} %rhs_hbm.1) | copy-start | bytes 393220
  6.0 0.7 %copy-start.5 = (s32[2,128]{1,0:T(2,128)S(1)}, s32[2,128]{1,0:T(2,128)}, u32[]{:S(2)}) copy-start(s32[2,128]{1,0:T(2,128)} %cols_ref.1) | copy-start | bytes 3076
  6.7 0.7 %copy-start.6 = (s32[2,128]{1,0:T(2,128)S(1)}, s32[2,128]{1,0:T(2,128)}, u32[]{:S(2)}) copy-start(s32[2,128]{1,0:T(2,128)} %ccols_ref.1) | copy-start | bytes 3076
  7.3 0.7 copy-start.7

commit v2 on v0

v2 whole, which is shorter than its diff:
```python
import functools

import jax
import jax.numpy as jnp
from jax import lax
from jax.experimental import pallas as pl
from jax.experimental.pallas import tpu as pltpu
from jax.sharding import PartitionSpec as P

OMEGA = 0.7
S = 64
R = 4
GROUPS = 2
PAIR = R // GROUPS
C = 128
HALF = 64
ROWS = 16
SPAN = PAIR // 2 * S
RIMS = 5
FINE, COARSE = 0, 1
MESH = pl.DeviceIdType.MESH
F32 = jnp.float32
BF16 = jnp.bfloat16


def lane_low(rows):
    return lax.broadcasted_iota(jnp.int32, (rows, C), 1) < HALF


def fold_rows(parts):
    sub = lax.broadcasted_iota(jnp.int32, (8, C), 0)
    four = sub < 4
    two = lax.rem(sub, 4) < 2
    one = lax.rem(sub, 2) < 1
    level = [
        jnp.where(four, parts[i], parts[i + 4])
        + pltpu.roll(jnp.where(four, parts[i + 4], parts[i]), 4, 0)
        for i in range(4)
    ]
    level = [
        jnp.where(
            two,
            level[i] + pltpu.roll(level[i], 6, 0),
            level[i + 2] + pltpu.roll(level[i + 2], 2, 0),
        )
        for i in range(2)
    ]
    return jnp.where(
        one,
        level[0] + pltpu.roll(level[0], 7, 0),
        level[1] + pltpu.roll(level[1], 1, 0),
    )


def products(terms, start=None):
    sums = [[None] * PAIR for _ in range(8)] if start is None else start
    for load, vector in terms:
        for low in range(0, S, 8):
            pieces = [vector(r, low) for r in range(PAIR)]
            for i in range(8):
                matrix = load(i, low)
                for r in range(PAIR):
                    piece = matrix * pieces[r]
                    sums[i][r] = piece if sums[i][r] is None else sums[i][r] + piece
    return sums


def kernel(
    sizes,
    rhs_hbm, diag_hbm, off_hbm, cols_hbm, agg_hbm, cdiag_hbm, coff_hbm, ccols_hbm,
    out_hbm,
    cols_ref, agg_ref, ccols_ref, rhs_in, diag_in, off_in, diag, off_near, off_far, scale, fixed, field, q, u, xb, xw, near, far, acc,
    hot_near, hot_far, member,
    send_rim, get_rim, send_part, get_part, send_short, get_short,
    load_sem, save_sem, rim_send, rim_get, part_send, part_get, short_send, short_get,
):
    spaces, levels = sizes
    space = lax.axis_index("space")
    level = lax.axis_index("level")
    index = space * levels + level
    count = spaces * levels
    after = lax.rem(index + 1, count)
    before = lax.rem(index + count - 1, count)
    fine_next = (lax.div(after, levels), lax.rem(after, levels))
    fine_last = (lax.div(before, levels), lax.rem(before, levels))
    space_next = (lax.rem(space + 1, spaces), level)
    space_last = (lax.rem(space + spaces - 1, spaces), level)
    peers = [(space, lax.rem(level + k, levels)) for k in range(1, levels)]

    barrier = pltpu.get_barrier_semaphore()
    partners = [fine_next, fine_last, space_next, space_last] + peers
    for partner in partners:
        pl.semaphore_signal(barrier, inc=1, device_id=partner, device_id_type=MESH)

    def load(k, source, target):
        return pltpu.make_async_copy(source, target, load_sem.at[k])

    half = S // 2
    load_diag = [
        load(k, diag_hbm.at[k * half : (k + 1) * half], diag_in.at[FINE, k * half : (k + 1) * half])
        for k in range(2)
    ]
    load_rhs = load(2, rhs_hbm, rhs_in)
    load_cols = load(3, cols_hbm, cols_ref)
    load_off = [
        load(4 + k, off_hbm.at[k * half : (k + 1) * half], off_in.at[k * half : (k + 1) * half])
        for k in range(2)
    ]
    load_coarse = [
        load(6, agg_hbm, agg_ref),
        load(7, ccols_hbm, ccols_ref),
        load(8, cdiag_hbm, diag_in.at[COARSE]),
        load(9, coff_hbm, off_in.at[S : S + ROWS]),
    ]
    for copy in load_diag + [load_rhs, load_cols] + load_off + load_coarse:
        copy.start()

    def remote(source, target, sent, got, device):
        return pltpu.make_async_remote_copy(
            src_ref=source, dst_ref=target, send_sem=sent, recv_sem=got,
            device_id=device, device_id_type=MESH,
        )

    def rim_copies(rim, group, kind):
        targets = (fine_next, fine_last) if kind == FINE else (space_next, space_last)
        return [
            remote(
                send_rim.at[rim, group, k], get_rim.at[rim, group, k],
                rim_send.at[rim, group, k], rim_get.at[rim, group, k], targets[k],
            )
            for k in range(2)
        ]

    def part_copies(group):
        return [
            remote(
                send_part.at[group], get_part.at[group, k],
                part_send.at[group, k], part_get.at[group, k], peer,
            )
            for k, peer in enumerate(peers)
        ]

    def short_copies(sweep, group):
        return [
            remote(
                send_short.at[sweep, group], get_short.at[sweep, group, k],
                short_send.at[sweep, group, k], short_get.at[sweep, group, k], peer,
            )
            for k, peer in enumerate(peers)
        ]

    low_lane = lax.broadcasted_iota(jnp.int32, (1, C), 1) < HALF

    def one_hot(cells):
        return (lax.broadcasted_iota(jnp.int32, (C, C), 0) == cells).astype(F32).astype(BF16)

    def tables(kind, cols, first):
        place = cols - first
        own = jnp.where(low_lane, place[1:2], place[0:1])
        reach = jnp.where(low_lane, place[0:1], place[1:2])
        hot_near[kind] = one_hot(own)
        left = jnp.where(reach < 0, reach + HALF, -1)
        right = jnp.where(reach >= C, reach - HALF, -1)
        rim = jnp.maximum(left, right)
        swapped = jnp.where(rim < 0, rim, lax.rem(rim + HALF, C))
        hot_far[kind, 0] = one_hot(rim)
        hot_far[kind, 1] = one_hot(swapped)
        hot_far[kind, 2] = one_hot(reach)

    field[...] = jnp.zeros_like(field)

    def widen_diag(kind, start, stop):
        sub = lax.broadcasted_iota(jnp.int32, (8, C), 0)

        def step(block, carry):
            low = pl.multiple_of(block * 8, 8)
            total = jnp.zeros((8, C), F32)
            for i in range(8):
                diag[kind, low + i] = diag_in[kind, low + i].astype(F32)
                total = jnp.where(sub == i, diag[kind, low + i, pl.ds(low, 8), :], total)
            scale[kind, pl.ds(low, 8), :] = 1.0 / total
            return carry

        lax.fori_loop(start // 8, stop // 8, step, 0)

    def widen_off(target, first, start, stop):
        mask = lane_low(S)

        def step(block, carry):
            for i in range(4):
                row = start + block * 4 + i
                target[row] = jnp.where(mask, off_in[row, first], off_in[row, 1 - first]).astype(F32)
            return carry

        lax.fori_loop(0, (stop - start) // 4, step, 0)

    def smooth(kind, group):
        for r in range(PAIR):
            u[r] = q[group, r] * scale[kind]

        def step(block, carry):
            base = block * 8
            sums = products(
                [
                    (
                        lambda i, low: diag[kind, base + i, low : low + 8, :],
                        lambda r, low: u[r, low : low + 8, :],
                    )
                ]
            )
            rows = pl.ds(pl.multiple_of(base, 8), 8)
            for r in range(PAIR):
                total = fold_rows([sums[i][r] for i in range(8)])
                change = (OMEGA * scale[kind, rows, :]) * (2.0 * q[group, r, rows, :] - total)
                field[kind, group, r, rows, :] = field[kind, group, r, rows, :] + change
            return carry

        lax.fori_loop(0, S // 8, step, 0)

    def start_rims(rim, group, kind):
        rounded = field[kind, group].astype(BF16)
        xb[group] = rounded
        xw[group] = rounded.astype(F32)
        lower = pltpu.roll(field[kind, group, : PAIR // 2].reshape(SPAN, C), HALF, 1)
        upper = field[kind, group, PAIR // 2 :].reshape(SPAN, C)
        mask = lane_low(SPAN)
        send_rim[rim, group, 0] = jnp.where(mask, lower, upper).astype(BF16)
        send_rim[rim, group, 1] = jnp.where(mask, upper, lower).astype(BF16)
        for copy in rim_copies(rim, group, kind):
            copy.start()

    def place(kind):
        return (0, 0, S) if kind == FINE else (level * ROWS, S, ROWS)

    def apply_near(group, kind):
        near[...] = jnp.dot(
            xb[group].reshape(PAIR * S, C), hot_near[kind], preferred_element_type=F32
        ).reshape(PAIR, S, C)
        start, first, rows = place(kind)

        def step(block, carry):
            base = block * 8
            sums = products(
                [
                    (
                        lambda i, low: diag[kind, start + base + i, low : low + 8, :],
                        lambda r, low: xw[group, r, low : low + 8, :],
                    ),
                    (
                        lambda i, low: off_near[first + base + i, low : low + 8, :],
                        lambda r, low: near[r, low : low + 8, :],
                    ),
                ]
            )
            for i in range(8):
                for r in range(PAIR):
                    acc[group, block, i * PAIR + r] = sums[i][r]
            return carry

        lax.fori_loop(0, rows // 8, step, 0)

    def finish_rims(rim, group, kind):
        for copy in rim_copies(rim, group, kind):
            copy.wait_recv()
        left = get_rim[rim, group, 0]
        right = get_rim[rim, group, 1]
        mask = lane_low(SPAN)
        for k in range(2):
            own = slice(k * PAIR // 2, (k + 1) * PAIR // 2)
            ends = jnp.where(mask, left, right) if k == 0 else jnp.where(mask, right, left)
            value = jnp.dot(ends, hot_far[kind, k], preferred_element_type=F32)
            value = value + jnp.dot(
                xb[group, own].reshape(SPAN, C), hot_far[kind, 2], preferred_element_type=F32
            )
            far[own] = value.reshape(PAIR // 2, S, C)
        start, first, count = place(kind)

        def step(block, carry):
            base = block * 8
            held = [[acc[group, block, i * PAIR + r] for r in range(PAIR)] for i in range(8)]
            sums = products(
                [
                    (
                        lambda i, low: off_far[first + base + i, low : low + 8, :],
                        lambda r, low: far[r, low : low + 8, :],
                    )
                ],
                held,
            )
            rows = pl.ds(pl.multiple_of(start + base, 8), 8)
            for r in range(PAIR):
                total = fold_rows([sums[i][r] for i in range(8)])
                q[group, r, rows, :] = fixed[kind, group, r, rows, :] - total
            return carry

        lax.fori_loop(0, count // 8, step, 0)

    def split_dot(value, dims):
        high = value.astype(BF16)
        low = (value - high.astype(F32)).astype(BF16)
        return sum(
            lax.dot_general(part, member[...], (dims, ((), ())), preferred_element_type=F32)
            for part in (high, low)
        )

    own_rows = pl.ds(pl.multiple_of(level * ROWS, ROWS), ROWS)

    def send_residual(group):
        part = split_dot(q[group].reshape(PAIR * S, C), ((1,), (1,)))
        send_part[group] = part.astype(BF16)
        for copy in part_copies(group):
            copy.start()

    def sum_residual(group):
        for copy in part_copies(group):
            copy.wait_recv()
        total = send_part[group].astype(F32)
        for k in range(levels - 1):
            total = total + get_part[group, k].astype(F32)
        fixed[COARSE, group] = total.reshape(PAIR, S, C)
        q[group] = total.reshape(PAIR, S, C)

    def send_shortfall(sweep, group):
        for r in range(PAIR):
            value = q[group, r, own_rows, :].astype(BF16)
            send_short[sweep, group, r] = value
            q[group, r, own_rows, :] = value.astype(F32)
        for copy in short_copies(sweep, group):
            copy.start()

    def join_shortfall(sweep, group):
        for k, copy in enumerate(short_copies(sweep, group)):
            copy.wait_recv()
            source = lax.rem(level + levels - (k + 1), levels)
            rows = pl.ds(pl.multiple_of(source * ROWS, ROWS), ROWS)
            for r in range(PAIR):
                q[group, r, rows, :] = get_short[sweep, group, k, r].astype(F32)

    groups = range(GROUPS)

    def save(group):
        own = slice(group * PAIR, (group + 1) * PAIR)
        return pltpu.make_async_copy(field.at[FINE, group], out_hbm.at[own], save_sem.at[group])

    for k in range(2):
        load_diag[k].wait()
        widen_diag(FINE, k * half, (k + 1) * half)
    load_rhs.wait()
    for r in range(R):
        value = rhs_in[:, r, :]
        fixed[FINE, r // PAIR, r % PAIR] = value
        q[r // PAIR, r % PAIR] = value
    for group in groups:
        smooth(FINE, group)
        if group == 0:
            pl.semaphore_wait(barrier, len(partners))
        start_rims(0, group, FINE)
    load_cols.wait()
    tables(FINE, cols_ref[...], index * C)
    for k in range(2):
        load_off[k].wait()
        widen_off(off_near, 1, k * half, (k + 1) * half)
    for group in groups:
        apply_near(group, FINE)
    widen_off(off_far, 0, 0, S)
    for copy in load_coarse:
        copy.wait()
    member[...] = one_hot(agg_ref[...] - space * C)
    for group in groups:
        finish_rims(0, group, FINE)
        smooth(FINE, group)
        start_rims(1, group, FINE)
        apply_near(group, FINE)
    for group in groups:
        finish_rims(1, group, FINE)
        send_residual(group)
    tables(COARSE, ccols_ref[...], space * C)
    widen_diag(COARSE, 0, S)
    widen_off(off_near, 1, S, S + ROWS)
    widen_off(off_far, 0, S, S + ROWS)
    for group in groups:
        sum_residual(group)
        smooth(COARSE, group)
        start_rims(2, group, COARSE)
        apply_near(group, COARSE)
    for sweep in range(2):
        for group in groups:
            finish_rims(2 + sweep, group, COARSE)
            send_shortfall(sweep, group)
        for group in groups:
            join_shortfall(sweep, group)
            smooth(COARSE, group)
            if sweep == 0:
                start_rims(3, group, COARSE)
                apply_near(group, COARSE)
            else:
                spread = split_dot(field[COARSE, group].reshape(PAIR * S, C), ((1,), (0,)))
                field[FINE, group] = field[FINE, group] + spread.reshape(PAIR, S, C)
                start_rims(4, group, FINE)
                apply_near(group, FINE)
    for group in groups:
        finish_rims(4, group, FINE)
        smooth(FINE, group)
        save(group).start()
    for group in groups:
        save(group).wait()
        for rim in range(RIMS):
            for copy in rim_copies(rim, group, FINE):
                copy.wait_send()
        for copy in part_copies(group):
            copy.wait_send()
        for sweep in range(2):
            for copy in short_copies(sweep, group):
                copy.wait_send()


def local(sizes, rhs, fine_diag, fine_off, fine_cols, aggregates, coarse_diag, coarse_off, coarse_cols):
    others = sizes[1] - 1
    hbm = pl.BlockSpec(memory_space=pl.ANY)
    dma = pltpu.SemaphoreType.DMA
    result = pl.pallas_call(
        functools.partial(kernel, sizes),
        out_shape=jax.ShapeDtypeStruct((R, S, C), F32),
        in_specs=[hbm] * 8,
        out_specs=hbm,
        scratch_shapes=[
            pltpu.VMEM((2, C), jnp.int32),
            pltpu.VMEM((1, C), jnp.int32),
            pltpu.VMEM((2, C), jnp.int32),
            pltpu.VMEM((S, R, C), F32),
            pltpu.VMEM((2, S, S, C), BF16),
            pltpu.VMEM((S + ROWS, 2, S, C), BF16),
            pltpu.VMEM((2, S, S, C), F32),
            pltpu.VMEM((S + ROWS, S, C), F32),
            pltpu.VMEM((S + ROWS, S, C), F32),
            pltpu.VMEM((2, S, C), F32),
            pltpu.VMEM((2, GROUPS, PAIR, S, C), F32),
            pltpu.VMEM((2, GROUPS, PAIR, S, C), F32),
            pltpu.VMEM((GROUPS, PAIR, S, C), F32),
            pltpu.VMEM((PAIR, S, C), F32),
            pltpu.VMEM((GROUPS, PAIR, S, C), BF16),
            pltpu.VMEM((GROUPS, PAIR, S, C), F32),
            pltpu.VMEM((PAIR, S, C), F32),
            pltpu.VMEM((PAIR, S, C), F32),
            pltpu.VMEM((GROUPS, S // 8, 8 * PAIR, 8, C), F32),
            pltpu.VMEM((2, C, C), BF16),
            pltpu.VMEM((2, 3, C, C), BF16),
            pltpu.VMEM((C, C), BF16),
            pltpu.VMEM((RIMS, GROUPS, 2, SPAN, C), BF16),
            pltpu.VMEM((RIMS, GROUPS, 2, SPAN, C), BF16),
            pltpu.VMEM((GROUPS, PAIR * S, C), BF16),
            pltpu.VMEM((GROUPS, others, PAIR * S, C), BF16),
            pltpu.VMEM((2, GROUPS, PAIR, ROWS, C), BF16),
            pltpu.VMEM((2, GROUPS, others, PAIR, ROWS, C), BF16),
            dma((10,)),
            dma((GROUPS,)),
            dma((RIMS, GROUPS, 2)),
            dma((RIMS, GROUPS, 2)),
            dma((GROUPS, others)),
            dma((GROUPS, others)),
            dma((2, GROUPS, others)),
            dma((2, GROUPS, others)),
        ],
        compiler_params=pltpu.CompilerParams(
            collective_id=0, has_side_effects=True, vmem_limit_bytes=63 * 1024 * 1024
        ),
        name="vcycle",
    )(
        rhs, fine_diag, fine_off, fine_cols, aggregates.reshape(1, C),
        coarse_diag, coarse_off, coarse_cols,
    )
    return result.transpose(1, 0, 2)


def solution(mesh):
    placed = (
        P(None, None, ("space", "level")),
        P(None, None, ("space", "level")),
        P(None, None, None, ("space", "level")),
        P(None, ("space", "level")),
        P(("space", "level")),
        P(None, None, "space"),
        P("level", None, None, "space"),
        P(None, "space"),
    )
    sizes = (mesh.shape["space"], mesh.shape["level"])
    return jax.shard_map(
        functools.partial(local, sizes),
        mesh=mesh,
        in_specs=placed,
        out_specs=P(None, None, ("space", "level")),
        check_vma=False,
    )
```

time: 285 us -> 56.5 us (0.20)
  the two profiles are of different devices: /device:TPU:127 before, /device:TPU:1 now
where the time goes in v2:
time: 56.5 us; the launch traced here: 56.4 us
  Pallas kernels  54.7 us (97%)
  local copies, waits for them, and re-layouts  1.65 us (3%)
    pallas_call x1, Pallas kernels, local(): pl.pallas_call(functools.partial(kernel, sizes), out_shape=jax.ShapeDtype...  54.7 us
    transpose x1, local copies, waits for them, and re-layouts, local(): return result.transpose(1, 0, 2)  1.65 us

profile of v2, /device:TPU:1, one launch (start us, length us, event | category | flops | bytes accessed | tf_op | source)
XLA Modules:
  0.0 56.4 jit_solution(14120152281288378534)
XLA Ops:
  0.0 54.7 %vcycle.1 = f32[4,64,128]{2,1,0:T(8,128)} custom-call(f32[64,4,128]{2,1,0:T(4,128)} %rhs_hbm.1, bf16[64,64,128]{2,1,0:T(8,128)(2,1)} %diag_hbm.1, bf16[64,2,64,128]{3,2,1,0:T(8,128)(2,1)} %off_hbm.1, s32[2,128]{1,0:T(2,128)} %cols_hbm.1, s32[1,128]{1,0:T(1,128)} %bitcast.3, bf16[64,64,128]{2,1,0:T(8,128)(2,1)} %cdiag_hbm.1, ...), custom_call_target="tpu_custom_call" | custom-call | tf_op jit(solution)/shard_map/vcycle/pallas_call | solution.py:421
  54.7 1.6 %copy.9 = f32[64,4,128]{2,1,0:T(4,128)} copy(f32[64,4,128]{2,0,1:T(8,128)} %bitcast.2) | data formatting | bytes 262144 | tf_op jit(solution)/shard_map/transpose | solution.py:472

commit v3 on v2

--- a/solution.py
+++ b/solution.py
@@ -16,8 +16,8 @@
 HALF = 64
 ROWS = 16
 SPAN = PAIR // 2 * S
-RIMS = 5
 FINE, COARSE = 0, 1
+RIM_KINDS = (FINE, FINE, COARSE, COARSE, FINE)
 MESH = pl.DeviceIdType.MESH
 F32 = jnp.float32
 BF16 = jnp.bfloat16
@@ -87,10 +87,24 @@
     space_last = (lax.rem(space + spaces - 1, spaces), level)
     peers = [(space, lax.rem(level + k, levels)) for k in range(1, levels)]
 
+    beyond = {
+        FINE: (index < count - 1, index > 0),
+        COARSE: (space < spaces - 1, space > 0),
+    }
+    targets = {FINE: (fine_next, fine_last), COARSE: (space_next, space_last)}
+
     barrier = pltpu.get_barrier_semaphore()
-    partners = [fine_next, fine_last, space_next, space_last] + peers
-    for partner in partners:
+    awaited = levels - 1
+
+    def greet(partner):
         pl.semaphore_signal(barrier, inc=1, device_id=partner, device_id_type=MESH)
+
+    for partner in peers:
+        greet(partner)
+    for kind in (FINE, COARSE):
+        for k in range(2):
+            awaited = awaited + beyond[kind][k].astype(jnp.int32)
+            pl.when(beyond[kind][k])(functools.partial(greet, targets[kind][k]))
 
     def load(k, source, target):
         return pltpu.make_async_copy(source, target, load_sem.at[k])
@@ -122,11 +136,10 @@
         )
 
     def rim_copies(rim, group, kind):
-        targets = (fine_next, fine_last) if kind == FINE else (space_next, space_last)
         return [
             remote(
                 send_rim.at[rim, group, k], get_rim.at[rim, group, k],
-                rim_send.at[rim, group, k], rim_get.at[rim, group, k], targets[k],
+                rim_send.at[rim, group, k], rim_get.at[rim, group, k], targets[kind][k],
             )
             for k in range(2)
         ]
@@ -169,6 +182,15 @@
 
     field[...] = jnp.zeros_like(field)
 
+    def clear(kind, k):
+        for rim in range(len(RIM_KINDS)):
+            if RIM_KINDS[rim] == kind:
+                get_rim[rim, :, k] = jnp.zeros((GROUPS, SPAN, C), BF16)
+
+    for kind in (FINE, COARSE):
+        for k in range(2):
+            pl.when(~beyond[kind][1 - k])(functools.partial(clear, kind, k))
+
     def widen_diag(kind, start, stop):
         sub = lax.broadcasted_iota(jnp.int32, (8, C), 0)
 
@@ -226,8 +248,8 @@
         mask = lane_low(SPAN)
         send_rim[rim, group, 0] = jnp.where(mask, lower, upper).astype(BF16)
         send_rim[rim, group, 1] = jnp.where(mask, upper, lower).astype(BF16)
-        for copy in rim_copies(rim, group, kind):
-            copy.start()
+        for k, copy in enumerate(rim_copies(rim, group, kind)):
+            pl.when(beyond[kind][k])(copy.start)
 
     def place(kind):
         return (0, 0, S) if kind == FINE else (level * ROWS, S, ROWS)
@@ -260,8 +282,8 @@
         lax.fori_loop(0, rows // 8, step, 0)
 
     def finish_rims(rim, group, kind):
-        for copy in rim_copies(rim, group, kind):
-            copy.wait_recv()
+        for k, copy in enumerate(rim_copies(rim, group, kind)):
+            pl.when(beyond[kind][1 - k])(copy.wait_recv)
         left = get_rim[rim, group, 0]
         right = get_rim[rim, group, 1]
         mask = lane_low(SPAN)
@@ -353,7 +375,7 @@
     for group in groups:
         smooth(FINE, group)
         if group == 0:
-            pl.semaphore_wait(barrier, len(partners))
+            pl.semaphore_wait(barrier, awaited)
         start_rims(0, group, FINE)
     load_cols.wait()
     tables(FINE, cols_ref[...], index * C)
@@ -404,9 +426,10 @@
         save(group).start()
     for group in groups:
         save(group).wait()
-        for rim in range(RIMS):
-            for copy in rim_copies(rim, group, FINE):
-                copy.wait_send()
+        for rim in range(len(RIM_KINDS)):
+            kind = RIM_KINDS[rim]
+            for k, copy in enumerate(rim_copies(rim, group, kind)):
+                pl.when(beyond[kind][k])(copy.wait_send)
         for copy in part_copies(group):
             copy.wait_send()
         for sweep in range(2):
@@ -446,16 +469,16 @@
             pltpu.VMEM((2, C, C), BF16),
             pltpu.VMEM((2, 3, C, C), BF16),
             pltpu.VMEM((C, C), BF16),
-            pltpu.VMEM((RIMS, GROUPS, 2, SPAN, C), BF16),
-            pltpu.VMEM((RIMS, GROUPS, 2, SPAN, C), BF16),
+            pltpu.VMEM((len(RIM_KINDS), GROUPS, 2, SPAN, C), BF16),
+            pltpu.VMEM((len(RIM_KINDS), GROUPS, 2, SPAN, C), BF16),
             pltpu.VMEM((GROUPS, PAIR * S, C), BF16),
             pltpu.VMEM((GROUPS, others, PAIR * S, C), BF16),
             pltpu.VMEM((2, GROUPS, PAIR, ROWS, C), BF16),
             pltpu.VMEM((2, GROUPS, others, PAIR, ROWS, C), BF16),
             dma((10,)),
             dma((GROUPS,)),
-            dma((RIMS, GROUPS, 2)),
-            dma((RIMS, GROUPS, 2)),
+            dma((len(RIM_KINDS), GROUPS, 2)),
+            dma((len(RIM_KINDS), GROUPS, 2)),
             dma((GROUPS, others)),
             dma((GROUPS, others)),
             dma((2, GROUPS, others)),

time: 56.5 us -> 48.4 us (0.86)
  the two profiles are of different devices: /device:TPU:1 before, /device:TPU:385 now
where the time goes in v3:
time: 48.4 us; the launch traced here: 48.3 us
  Pallas kernels  46.6 us (96%)
  local copies, waits for them, and re-layouts  1.65 us (3%)
    pallas_call x1, Pallas kernels, local(): pl.pallas_call(functools.partial(kernel, sizes), out_shape=jax.ShapeDtype...  46.6 us
    transpose x1, local copies, waits for them, and re-layouts, local(): return result.transpose(1, 0, 2)  1.65 us

profile of v3, /device:TPU:385, one launch (start us, length us, event | category | flops | bytes accessed | tf_op | source)
XLA Modules:
  0.0 48.3 jit_solution(4598847397993086787)
XLA Ops:
  0.0 46.6 %vcycle.1 = f32[4,64,128]{2,1,0:T(8,128)} custom-call(f32[64,4,128]{2,1,0:T(4,128)} %rhs_hbm.1, bf16[64,64,128]{2,1,0:T(8,128)(2,1)} %diag_hbm.1, bf16[64,2,64,128]{3,2,1,0:T(8,128)(2,1)} %off_hbm.1, s32[2,128]{1,0:T(2,128)} %cols_hbm.1, s32[1,128]{1,0:T(1,128)} %bitcast.3, bf16[64,64,128]{2,1,0:T(8,128)(2,1)} %cdiag_hbm.1, ...), custom_call_target="tpu_custom_call" | custom-call | tf_op jit(solution)/shard_map/vcycle/pallas_call | solution.py:444
  46.6 1.6 %copy.9 = f32[64,4,128]{2,1,0:T(4,128)} copy(f32[64,4,128]{2,0,1:T(8,128)} %bitcast.2) | data formatting | bytes 262144 | tf_op jit(solution)/shard_map/transpose | solution.py:495

commit v4 on v3

--- a/solution.py
+++ b/solution.py
@@ -15,7 +15,8 @@
 C = 128
 HALF = 64
 ROWS = 16
-SPAN = PAIR // 2 * S
+PIECE = 4
+SPAN = PAIR * S // 2
 FINE, COARSE = 0, 1
 RIM_KINDS = (FINE, FINE, COARSE, COARSE, FINE)
 MESH = pl.DeviceIdType.MESH
@@ -71,8 +72,8 @@
     out_hbm,
     cols_ref, agg_ref, ccols_ref, rhs_in, diag_in, off_in, diag, off_near, off_far, scale, fixed, field, q, u, xb, xw, near, far, acc,
     hot_near, hot_far, member,
-    send_rim, get_rim, send_part, get_part, send_short, get_short,
-    load_sem, save_sem, rim_send, rim_get, part_send, part_get, short_send, short_get,
+    send_rim, get_rim, send_part, get_part, send_short, get_short, send_far, get_far,
+    load_sem, save_sem, rim_send, rim_get, part_send, part_get, short_send, short_get, far_send, far_get,
 ):
     spaces, levels = sizes
     space = lax.axis_index("space")
@@ -93,6 +94,8 @@
     }
     targets = {FINE: (fine_next, fine_last), COARSE: (space_next, space_last)}
 
+    far_first = sorted(range(levels - 1), key=lambda k: -min(k + 1, levels - 1 - k))
+
     barrier = pltpu.get_barrier_semaphore()
     awaited = levels - 1
 
@@ -120,13 +123,13 @@
         load(4 + k, off_hbm.at[k * half : (k + 1) * half], off_in.at[k * half : (k + 1) * half])
         for k in range(2)
     ]
+    load_coff = load(9, coff_hbm, off_in.at[S : S + ROWS])
     load_coarse = [
         load(6, agg_hbm, agg_ref),
         load(7, ccols_hbm, ccols_ref),
         load(8, cdiag_hbm, diag_in.at[COARSE]),
-        load(9, coff_hbm, off_in.at[S : S + ROWS]),
     ]
-    for copy in load_diag + [load_rhs, load_cols] + load_off + load_coarse:
+    for copy in load_diag + [load_rhs, load_coff, load_cols] + load_off + load_coarse:
         copy.start()
 
     def remote(source, target, sent, got, device):
@@ -161,6 +164,24 @@
             )
             for k, peer in enumerate(peers)
         ]
+
+    def far_copies(piece):
+        rows = slice(piece * PIECE, (piece + 1) * PIECE)
+        return [
+            remote(
+                send_far.at[rows], get_far.at[k, rows],
+                far_send.at[piece, k], far_get.at[piece, k], peer,
+            )
+            for k, peer in enumerate(peers)
+        ]
+
+    def start_far(piece):
+        for k in far_first:
+            far_copies(piece)[k].start()
+
+    def source_rows(k, first=0):
+        source = lax.rem(level + levels - (k + 1), levels)
+        return first + pl.multiple_of(source * ROWS, ROWS)
 
     low_lane = lax.broadcasted_iota(jnp.int32, (1, C), 1) < HALF
 
@@ -216,9 +237,10 @@
 
         lax.fori_loop(0, (stop - start) // 4, step, 0)
 
-    def smooth(kind, group):
-        for r in range(PAIR):
-            u[r] = q[group, r] * scale[kind]
+    def smooth(kind, group, scaled=False):
+        if not scaled:
+            for r in range(PAIR):
+                u[r] = q[group, r] * scale[kind]
 
         def step(block, carry):
             base = block * 8
@@ -237,28 +259,24 @@
                 field[kind, group, r, rows, :] = field[kind, group, r, rows, :] + change
             return carry
 
-        lax.fori_loop(0, S // 8, step, 0)
+        lax.fori_loop(0, S // 8, step, 0, unroll=2)
 
     def start_rims(rim, group, kind):
-        rounded = field[kind, group].astype(BF16)
-        xb[group] = rounded
-        xw[group] = rounded.astype(F32)
-        lower = pltpu.roll(field[kind, group, : PAIR // 2].reshape(SPAN, C), HALF, 1)
-        upper = field[kind, group, PAIR // 2 :].reshape(SPAN, C)
+        whole = field[kind, group].reshape(PAIR * S, C)
+        lower = pltpu.roll(whole[:SPAN], HALF, 1)
+        upper = whole[SPAN:]
         mask = lane_low(SPAN)
         send_rim[rim, group, 0] = jnp.where(mask, lower, upper).astype(BF16)
         send_rim[rim, group, 1] = jnp.where(mask, upper, lower).astype(BF16)
         for k, copy in enumerate(rim_copies(rim, group, kind)):
             pl.when(beyond[kind][k])(copy.start)
 
-    def place(kind):
-        return (0, 0, S) if kind == FINE else (level * ROWS, S, ROWS)
-
     def apply_near(group, kind):
-        near[...] = jnp.dot(
-            xb[group].reshape(PAIR * S, C), hot_near[kind], preferred_element_type=F32
-        ).reshape(PAIR, S, C)
-        start, first, rows = place(kind)
+        rounded = field[kind, group].astype(BF16)
+        xb[group] = rounded.reshape(PAIR * S, C)
+        xw[group] = rounded.astype(F32)
+        near[...] = jnp.dot(xb[group], hot_near[kind], preferred_element_type=F32).reshape(PAIR, S, C)
+        start, first, rows = (0, 0, S) if kind == FINE else (level * ROWS, S, ROWS)
 
         def step(block, carry):
             base = block * 8
@@ -274,12 +292,21 @@
                     ),
                 ]
             )
-            for i in range(8):
-                for r in range(PAIR):
-                    acc[group, block, i * PAIR + r] = sums[i][r]
-            return carry
-
-        lax.fori_loop(0, rows // 8, step, 0)
+            if kind == FINE:
+                for i in range(8):
+                    for r in range(PAIR):
+                        acc[group, block, i * PAIR + r] = sums[i][r]
+                return carry
+            place = pl.ds(pl.multiple_of(start + base, 8), 8)
+            for r in range(PAIR):
+                total = fold_rows([sums[i][r] for i in range(8)])
+                q[group, r, place, :] = fixed[kind, group, r, place, :] - total
+            return carry
+
+        lax.fori_loop(0, rows // 8, step, 0, unroll=2)
+
+    def gather_own(group, kind):
+        far[group] = jnp.dot(xb[group], hot_far[kind, 2], preferred_element_type=F32)
 
     def finish_rims(rim, group, kind):
         for k, copy in enumerate(rim_copies(rim, group, kind)):
@@ -288,34 +315,37 @@
         right = get_rim[rim, group, 1]
         mask = lane_low(SPAN)
         for k in range(2):
-            own = slice(k * PAIR // 2, (k + 1) * PAIR // 2)
+            own = slice(k * SPAN, (k + 1) * SPAN)
             ends = jnp.where(mask, left, right) if k == 0 else jnp.where(mask, right, left)
-            value = jnp.dot(ends, hot_far[kind, k], preferred_element_type=F32)
-            value = value + jnp.dot(
-                xb[group, own].reshape(SPAN, C), hot_far[kind, 2], preferred_element_type=F32
-            )
-            far[own] = value.reshape(PAIR // 2, S, C)
-        start, first, count = place(kind)
+            far[group, own] = far[group, own] + jnp.dot(
+                ends, hot_far[kind, k], preferred_element_type=F32
+            )
+        first = 0 if kind == FINE else S
 
         def step(block, carry):
             base = block * 8
-            held = [[acc[group, block, i * PAIR + r] for r in range(PAIR)] for i in range(8)]
+            held = None
+            if kind == FINE:
+                held = [[acc[group, block, i * PAIR + r] for r in range(PAIR)] for i in range(8)]
             sums = products(
                 [
                     (
                         lambda i, low: off_far[first + base + i, low : low + 8, :],
-                        lambda r, low: far[r, low : low + 8, :],
+                        lambda r, low: far[group, r * S + low : r * S + low + 8],
                     )
                 ],
                 held,
             )
-            rows = pl.ds(pl.multiple_of(start + base, 8), 8)
+            rows = pl.ds(pl.multiple_of(base, 8), 8)
             for r in range(PAIR):
                 total = fold_rows([sums[i][r] for i in range(8)])
-                q[group, r, rows, :] = fixed[kind, group, r, rows, :] - total
-            return carry
-
-        lax.fori_loop(0, count // 8, step, 0)
+                known = fixed[kind, group, r, rows, :] if kind == FINE else q[group, r, rows, :]
+                value = known - total
+                q[group, r, rows, :] = value
+                u[r, rows, :] = value * scale[kind, rows, :]
+            return carry
+
+        lax.fori_loop(0, S // 8, step, 0, unroll=2)
 
     def split_dot(value, dims):
         high = value.astype(BF16)
@@ -330,8 +360,8 @@
     def send_residual(group):
         part = split_dot(q[group].reshape(PAIR * S, C), ((1,), (1,)))
         send_part[group] = part.astype(BF16)
-        for copy in part_copies(group):
-            copy.start()
+        for k in far_first:
+            part_copies(group)[k].start()
 
     def sum_residual(group):
         for copy in part_copies(group):
@@ -347,16 +377,39 @@
             value = q[group, r, own_rows, :].astype(BF16)
             send_short[sweep, group, r] = value
             q[group, r, own_rows, :] = value.astype(F32)
-        for copy in short_copies(sweep, group):
-            copy.start()
+        for k in far_first:
+            short_copies(sweep, group)[k].start()
 
     def join_shortfall(sweep, group):
         for k, copy in enumerate(short_copies(sweep, group)):
             copy.wait_recv()
-            source = lax.rem(level + levels - (k + 1), levels)
-            rows = pl.ds(pl.multiple_of(source * ROWS, ROWS), ROWS)
+            rows = pl.ds(source_rows(k), ROWS)
             for r in range(PAIR):
                 q[group, r, rows, :] = get_short[sweep, group, k, r].astype(F32)
+
+    def pick_far():
+        mask = lane_low(S)
+
+        def step(row, carry):
+            send_far[row] = jnp.where(mask, off_in[S + row, 0], off_in[S + row, 1])
+            return carry
+
+        lax.fori_loop(0, ROWS, step, 0, unroll=4)
+
+    def join_far():
+        for piece in range(ROWS // PIECE):
+            for copy in far_copies(piece):
+                copy.wait_recv()
+
+        def step(block, carry):
+            for i in range(4):
+                row = block * 4 + i
+                off_far[S + level * ROWS + row] = send_far[row].astype(F32)
+                for k in range(levels - 1):
+                    off_far[source_rows(k, S) + row] = get_far[k, row].astype(F32)
+            return carry
+
+        lax.fori_loop(0, ROWS // 4, step, 0)
 
     groups = range(GROUPS)
 
@@ -377,6 +430,9 @@
         if group == 0:
             pl.semaphore_wait(barrier, awaited)
         start_rims(0, group, FINE)
+    load_coff.wait()
+    pick_far()
+    start_far(0)
     load_cols.wait()
     tables(FINE, cols_ref[...], index * C)
     for k in range(2):
@@ -384,46 +440,62 @@
         widen_off(off_near, 1, k * half, (k + 1) * half)
     for group in groups:
         apply_near(group, FINE)
+        gather_own(group, FINE)
     widen_off(off_far, 0, 0, S)
     for copy in load_coarse:
         copy.wait()
     member[...] = one_hot(agg_ref[...] - space * C)
     for group in groups:
         finish_rims(0, group, FINE)
-        smooth(FINE, group)
+        smooth(FINE, group, scaled=True)
         start_rims(1, group, FINE)
+    start_far(1)
+    for group in groups:
         apply_near(group, FINE)
+        gather_own(group, FINE)
     for group in groups:
         finish_rims(1, group, FINE)
         send_residual(group)
+    start_far(2)
+    start_far(3)
     tables(COARSE, ccols_ref[...], space * C)
     widen_diag(COARSE, 0, S)
     widen_off(off_near, 1, S, S + ROWS)
-    widen_off(off_far, 0, S, S + ROWS)
     for group in groups:
         sum_residual(group)
         smooth(COARSE, group)
         start_rims(2, group, COARSE)
         apply_near(group, COARSE)
-    for sweep in range(2):
-        for group in groups:
-            finish_rims(2 + sweep, group, COARSE)
-            send_shortfall(sweep, group)
-        for group in groups:
-            join_shortfall(sweep, group)
-            smooth(COARSE, group)
-            if sweep == 0:
-                start_rims(3, group, COARSE)
-                apply_near(group, COARSE)
-            else:
-                spread = split_dot(field[COARSE, group].reshape(PAIR * S, C), ((1,), (0,)))
-                field[FINE, group] = field[FINE, group] + spread.reshape(PAIR, S, C)
-                start_rims(4, group, FINE)
-                apply_near(group, FINE)
+        send_shortfall(0, group)
+    for group in groups:
+        gather_own(group, COARSE)
+    join_far()
+    for group in groups:
+        join_shortfall(0, group)
+        finish_rims(2, group, COARSE)
+        smooth(COARSE, group, scaled=True)
+        start_rims(3, group, COARSE)
+        apply_near(group, COARSE)
+        send_shortfall(1, group)
+    for group in groups:
+        gather_own(group, COARSE)
+    for group in groups:
+        join_shortfall(1, group)
+        finish_rims(3, group, COARSE)
+        smooth(COARSE, group, scaled=True)
+        spread = split_dot(field[COARSE, group].reshape(PAIR * S, C), ((1,), (0,)))
+        field[FINE, group] = field[FINE, group] + spread.reshape(PAIR, S, C)
+        start_rims(4, group, FINE)
+    for group in groups:
+        apply_near(group, FINE)
+        gather_own(group, FINE)
     for group in groups:
         finish_rims(4, group, FINE)
-        smooth(FINE, group)
+        smooth(FINE, group, scaled=True)
         save(group).start()
+    for piece in range(ROWS // PIECE):
+        for copy in far_copies(piece):
+            copy.wait_send()
     for group in groups:
         save(group).wait()
         for rim in range(len(RIM_KINDS)):
@@ -455,16 +527,16 @@
             pltpu.VMEM((S + ROWS, 2, S, C), BF16),
             pltpu.VMEM((2, S, S, C), F32),
             pltpu.VMEM((S + ROWS, S, C), F32),
-            pltpu.VMEM((S + ROWS, S, C), F32),
+            pltpu.VMEM((2 * S, S, C), F32),
             pltpu.VMEM((2, S, C), F32),
             pltpu.VMEM((2, GROUPS, PAIR, S, C), F32),
             pltpu.VMEM((2, GROUPS, PAIR, S, C), F32),
             pltpu.VMEM((GROUPS, PAIR, S, C), F32),
             pltpu.VMEM((PAIR, S, C), F32),
-            pltpu.VMEM((GROUPS, PAIR, S, C), BF16),
+            pltpu.VMEM((GROUPS, PAIR * S, C), BF16),
             pltpu.VMEM((GROUPS, PAIR, S, C), F32),
             pltpu.VMEM((PAIR, S, C), F32),
-            pltpu.VMEM((PAIR, S, C), F32),
+            pltpu.VMEM((GROUPS, PAIR * S, C), F32),
             pltpu.VMEM((GROUPS, S // 8, 8 * PAIR, 8, C), F32),
             pltpu.VMEM((2, C, C), BF16),
             pltpu.VMEM((2, 3, C, C), BF16),
@@ -475,6 +547,8 @@
             pltpu.VMEM((GROUPS, others, PAIR * S, C), BF16),
             pltpu.VMEM((2, GROUPS, PAIR, ROWS, C), BF16),
             pltpu.VMEM((2, GROUPS, others, PAIR, ROWS, C), BF16),
+            pltpu.VMEM((ROWS, S, C), BF16),
+            pltpu.VMEM((others, ROWS, S, C), BF16),
             dma((10,)),
             dma((GROUPS,)),
             dma((len(RIM_KINDS), GROUPS, 2)),
@@ -483,6 +557,8 @@
             dma((GROUPS, others)),
             dma((2, GROUPS, others)),
             dma((2, GROUPS, others)),
+            dma((ROWS // PIECE, others)),
+            dma((ROWS // PIECE, others)),
         ],
         compiler_params=pltpu.CompilerParams(
             collective_id=0, has_side_effects=True, vmem_limit_bytes=63 * 1024 * 1024

time: 48.4 us -> 44.2 us (0.913)
  the two profiles are of different devices: /device:TPU:385 before, /device:TPU:1 now
where the time goes in v4:
time: 44.2 us; the launch traced here: 43.3 us
  Pallas kernels  41.7 us (94%)
  local copies, waits for them, and re-layouts  1.65 us (4%)
    pallas_call x1, Pallas kernels, local(): pl.pallas_call(functools.partial(kernel, sizes), out_shape=jax.ShapeDtype...  41.7 us
    transpose x1, local copies, waits for them, and re-layouts, local(): return result.transpose(1, 0, 2)  1.65 us

profile of v4, /device:TPU:1, one launch (start us, length us, event | category | flops | bytes accessed | tf_op | source)
XLA Modules:
  0.0 43.3 jit_solution(7968761224131645396)
XLA Ops:
  0.0 41.7 %vcycle.1 = f32[4,64,128]{2,1,0:T(8,128)} custom-call(f32[64,4,128]{2,1,0:T(4,128)} %rhs_hbm.1, bf16[64,64,128]{2,1,0:T(8,128)(2,1)} %diag_hbm.1, bf16[64,2,64,128]{3,2,1,0:T(8,128)(2,1)} %off_hbm.1, s32[2,128]{1,0:T(2,128)} %cols_hbm.1, s32[1,128]{1,0:T(1,128)} %bitcast.3, bf16[64,64,128]{2,1,0:T(8,128)(2,1)} %cdiag_hbm.1, ...), custom_call_target="tpu_custom_call" | custom-call | tf_op jit(solution)/shard_map/vcycle/pallas_call | solution.py:516
  41.7 1.6 %copy.9 = f32[64,4,128]{2,1,0:T(4,128)} copy(f32[64,4,128]{2,0,1:T(8,128)} %bitcast.2) | data formatting | bytes 262144 | tf_op jit(solution)/shard_map/transpose | solution.py:571

commit v5 on v4

--- a/solution.py
+++ b/solution.py
@@ -259,7 +259,7 @@
                 field[kind, group, r, rows, :] = field[kind, group, r, rows, :] + change
             return carry
 
-        lax.fori_loop(0, S // 8, step, 0, unroll=2)
+        lax.fori_loop(0, S // 8, step, 0, unroll=4)
 
     def start_rims(rim, group, kind):
         whole = field[kind, group].reshape(PAIR * S, C)
@@ -345,7 +345,7 @@
                 u[r, rows, :] = value * scale[kind, rows, :]
             return carry
 
-        lax.fori_loop(0, S // 8, step, 0, unroll=2)
+        lax.fori_loop(0, S // 8, step, 0, unroll=4)
 
     def split_dot(value, dims):
         high = value.astype(BF16)

time: 44.2 us -> 43.8 us (level)
  no operation moved by 1% of the time
where the time goes in v5:
time: 43.8 us; the launch traced here: 43 us
  Pallas kernels  41.4 us (95%)
  local copies, waits for them, and re-layouts  1.65 us (4%)
    pallas_call x1, Pallas kernels, local(): pl.pallas_call(functools.partial(kernel, sizes), out_shape=jax.ShapeDtype...  41.4 us
    transpose x1, local copies, waits for them, and re-layouts, local(): return result.transpose(1, 0, 2)  1.65 us

profile of v5, /device:TPU:1, one launch (start us, length us, event | category | flops | bytes accessed | tf_op | source)
XLA Modules:
  0.0 43.0 jit_solution(9891948828273265182)
XLA Ops:
  0.0 41.4 %vcycle.1 = f32[4,64,128]{2,1,0:T(8,128)} custom-call(f32[64,4,128]{2,1,0:T(4,128)} %rhs_hbm.1, bf16[64,64,128]{2,1,0:T(8,128)(2,1)} %diag_hbm.1, bf16[64,2,64,128]{3,2,1,0:T(8,128)(2,1)} %off_hbm.1, s32[2,128]{1,0:T(2,128)} %cols_hbm.1, s32[1,128]{1,0:T(1,128)} %bitcast.3, bf16[64,64,128]{2,1,0:T(8,128)(2,1)} %cdiag_hbm.1, ...), custom_call_target="tpu_custom_call" | custom-call | tf_op jit(solution)/shard_map/vcycle/pallas_call | solution.py:516
  41.4 1.6 %copy.9 = f32[64,4,128]{2,1,0:T(4,128)} copy(f32[64,4,128]{2,0,1:T(8,128)} %bitcast.2) | data formatting | bytes 262144 | tf_op jit(solution)/shard_map/transpose | solution.py:571
